TPU v7x, 256 devices: a whole 4x4x8 slice. The times are simulated.
256 devices in a mesh: orb: 4 (over z_hi), gx: 16 (over x, y), gy: 4 (over z_lo, core).
Axes of the slice: x: 4, y: 4, z: 8 (z_hi: 4, z_lo: 2; z = z_hi * 2 + z_lo), core: 2. Of those that a mesh axis runs over, the one named last changes fastest.
Arguments:
- orbitals: float32 [32, 160, 160, 128], P('orb', 'gx', 'gy'), may hold values from -1.6 to 1.6
- dielectric: float32 [160, 160, 128], P('gx', 'gy'), may hold values from 0.25 to 2
- owner_group: int32 [2], replicated, may hold values from 0 to 3, as said below
- block_slots: int32 [2, 4], replicated, may hold values from 0 to 7, as said below
Outputs:
- exchange: float32 [2, 4, 160, 160, 128], P(None, 'orb', 'gx', 'gy')
Inputs may be any that keep to these rules, and one draw needn't show every extreme that they name: `block_slots`: over all windows together, every slot 0 to 7 appears exactly once. `owner_group`: different windows have different owners.
All inputs are finite; a program needn't handle non-finite values.
Results may differ from a plain program's by a relative error of at most 0.00002.
Values sent between devices are 32-bit elements; how exact they have to be, the bound alone decides.
A program may use at most 192 MiB of HBM per device.

v0:
```python
import math

import jax
import jax.numpy as jnp
from jax import lax
from jax.sharding import PartitionSpec as P

FOUR_PI = 4.0 * math.pi
MIXING = 0.25
LOWEST = 0.5
HIGHEST = 24.0
SPECTRUM_MID = (HIGHEST + LOWEST) / 2.0
SPECTRUM_HALF = (HIGHEST - LOWEST) / 2.0
SPECTRUM_RATIO = SPECTRUM_MID / SPECTRUM_HALF
RATE_ZERO = 1.0 / SPECTRUM_RATIO
RATE_ONE = 1.0 / (2.0 * SPECTRUM_RATIO - RATE_ZERO)
RATE_TWO = 1.0 / (2.0 * SPECTRUM_RATIO - RATE_ONE)
KEEP_FACTORS = (RATE_ONE * RATE_ZERO, RATE_TWO * RATE_ONE)
STEP_FACTORS = (2.0 * RATE_ONE / SPECTRUM_HALF, 2.0 * RATE_TWO / SPECTRUM_HALF)


def with_halo(shard, sides, width):
    for axis, dim in sides:
        peers, length = (lax.axis_size(axis), shard.shape[dim])
        up = [(i, (i + 1) % peers) for i in range(peers)]
        down = [(j, i) for i, j in up]
        last = lax.slice_in_dim(shard, length - width, length, axis=dim)
        initial = lax.slice_in_dim(shard, 0, width, axis=dim)
        before = lax.ppermute(last, axis, up)
        after = lax.ppermute(initial, axis, down)
        shard = jnp.concatenate([before, shard, after], axis=dim)
    return shard


def broadcast(block, axis, owner):
    block = jnp.where(lax.axis_index(axis) == owner, block, jnp.zeros_like(block))
    return lax.psum(block, axis)


def operate(padded, coef_wide):
    center = padded[:, 1:-1, 1:-1, :]
    coef_mid = coef_wide[1:-1, 1:-1, :]
    neighbours = [
        (padded[:, 2:, 1:-1, :], coef_wide[2:, 1:-1, :]),
        (padded[:, :-2, 1:-1, :], coef_wide[:-2, 1:-1, :]),
        (padded[:, 1:-1, 2:, :], coef_wide[1:-1, 2:, :]),
        (padded[:, 1:-1, :-2, :], coef_wide[1:-1, :-2, :]),
    ]
    summed = jnp.zeros_like(center)
    for neighbour, coef_near in neighbours:
        summed = summed + 0.5 * (coef_mid + coef_near) * (center - neighbour)
    depth_pad = jnp.pad(center, ((0, 0), (0, 0), (0, 0), (1, 1)))
    coef_depth = jnp.pad(coef_mid, ((0, 0), (0, 0), (1, 1)), mode="edge")
    summed = summed + 0.5 * (coef_mid + coef_depth[:, :, 2:]) * (center - depth_pad[:, :, :, 2:])
    summed = summed + 0.5 * (coef_mid + coef_depth[:, :, :-2]) * (center - depth_pad[:, :, :, :-2])
    return summed


def smooth_iterate(source, coef_one):
    iterate = source / SPECTRUM_MID
    search = iterate
    for section in range(2):
        widened = with_halo(iterate, (("gx", 1), ("gy", 2)), 1)
        misfit = source - operate(widened, coef_one)
        search = KEEP_FACTORS[section] * search + STEP_FACTORS[section] * misfit
        iterate = iterate + search
    return iterate


def pair_sources(group, partners):
    members = group.shape[0]
    source = (FOUR_PI * group)[:, None] * partners[None]
    return source.reshape((members * partners.shape[0],) + partners.shape[1:])


def shards(orbitals, dielectric, owner_group, block_slots):
    resident_count = orbitals.shape[0]
    coef_wide = with_halo(dielectric, (("gx", 0), ("gy", 1)), 2)
    coef_one = coef_wide[1:-1, 1:-1, :]
    windows = block_slots.shape[0]
    results = []
    for window in range(windows):
        chosen = block_slots[window]
        picked = jnp.take(orbitals, chosen, axis=0)
        block_fields = broadcast(picked, "orb", owner_group[window])
        members = block_fields.shape[0]
        source = pair_sources(block_fields, orbitals)
        potential = smooth_iterate(source, coef_one)
        potential = potential.reshape((members, resident_count) + orbitals.shape[1:])
        partial_terms = jnp.sum(potential * orbitals[None], axis=1)
        results.append(lax.psum_scatter(partial_terms, "orb", scatter_dimension=0, tiled=True))
    summed = jnp.stack(results)
    return -MIXING * summed


def solution(mesh):
    in_specs = (P("orb", "gx", "gy", None), P("gx", "gy", None), P(), P())
    out_specs = P(None, "orb", "gx", "gy", None)
    return jax.shard_map(shards, mesh=mesh, in_specs=in_specs, out_specs=out_specs, check_vma=False)
```

profile of v0, /device:TPU:1, one launch (start us, length us, event | category | flops | bytes accessed | tf_op | source)
XLA Modules:
  0.0 325.8 jit_solution(3951149638046679509)
XLA Ops:
  6.5 1.4 fusion.109
  9.2 0.8 compare_and_fusion
  10.0 2.0 gather_fusion
  12.0 2.9 gather_fusion.1
  15.0 2.5 select_select_fusion
  17.5 0.0 all-reduce.7.cloned.1.call-update
  17.5 0.0 reduce-scatter.3.cloned.1.call-start
  17.6 0.6 fusion.107
  18.2 5.8 %collective-permute-start = (f32[2,40,128]{2,1,0:T(8,128)}, f32[2,40,128]{2,1,0:T(8,128)S(1)}, u32[]{:S(2)}, u32[]{:S(2)}) collective-permute-start(f32[2,40,128]{2,1,0:T(8,128)} %get-tuple-element.44), channel_id=1, source_target_pairs={{4,0},{8,4},{12,8},{16,12},{20,16},{24,20},{28,24},{32,28},{36,32}... | collective-permute-start | bytes 122888 | tf_op jit(solution)/shard_map/ppermute | solution.py:30
  24.0 0.1 fusion.108
  24.1 6.1 %collective-permute-done.2 = f32[2,40,128]{2,1,0:T(8,128)S(1)} collective-permute-done((f32[2,40,128]{2,1,0:T(8,128)S(1)}, f32[2,40,128]{2,1,0:T(8,128)S(1)}, u32[]{:S(2)}, u32[]{:S(2)}) %collective-permute-start.2) | collective-permute-done | bytes 40992 | tf_op jit(solution)/shard_map/ppermute | solution.py:29
  30.1 0.0 copy-start.8
  30.2 76.6 %all-reduce.7.cloned.1.call-done = (f32[4,10,40,128]{3,2,1,0:T(8,128)}, f32[4,10,40,128]{3,2,1,0:T(8,128)}) async-done(((f32[4,10,40,128]{3,2,1,0:T(8,128)}, f32[4,10,40,128]{3,2,1,0:T(8,128)}), (f32[4,10,40,128]{3,2,1,0:T(8,128)}, f32[4,10,40,128]{3,2,1,0:T(8,128)})) %all-reduce.7.cloned.1.call-update) | async-done | bytes 1638416 | tf_op jit(solution)/shard_map/psum | solution.py:37
  106.8 1.2 broadcast_multiply_fusion.3
  108.0 1.2 broadcast_multiply_fusion.2
  109.2 1.1 broadcast_multiply_fusion
  110.3 2.3 bitcast_multiply_fusion.1
  112.6 1.3 fusion.103
  113.9 1.1 collective-permute-start.13
  115.0 3.7 %collective-permute-start.12 = (f32[32,1,40,128]{3,0,2,1:T(8,128)}, f32[32,1,40,128]{3,0,2,1:T(8,128)S(1)}, u32[]{:S(2)}, u32[]{:S(2)}) collective-permute-start(f32[32,1,40,128]{3,0,2,1:T(8,128)} %get-tuple-element.29), channel_id=1, source_target_pairs={{4,0},{8,4},{12,8},{16,12},{20,16},{24,20},{28,24},{32,28},{36,32}... | collective-permute-start | bytes 1966088 | tf_op jit(solution)/shard_map/ppermute | solution.py:30
  118.7 2.3 bitcast_multiply_fusion.3
  121.0 0.1 fusion.105
  121.1 0.1 collective-permute-start.3
  121.2 4.8 %collective-permute-start.1 = (f32[32,1,40,128]{3,0,2,1:T(8,128)S(1)}, f32[32,1,40,128]{3,0,2,1:T(8,128)S(1)}, u32[]{:S(2)}, u32[]{:S(2)}) collective-permute-start(f32[32,1,40,128]{3,0,2,1:T(8,128)S(1)} %get-tuple-element.33), channel_id=1, source_target_pairs={{4,0},{8,4},{12,8},{16,12},{20,16},{24,20},{28,24},{32,28},{36,32}... | collective-permute-start | bytes 1966088 | tf_op jit(solution)/shard_map/ppermute | solution.py:30
  126.0 0.0 collective-permute-done
  126.0 2.1 collective-permute-start.4
  128.1 5.0 %collective-permute-done.13 = f32[32,1,40,128]{3,0,2,1:T(8,128)S(1)} collective-permute-done((f32[32,1,40,128]{3,0,2,1:T(8,128)}, f32[32,1,40,128]{3,0,2,1:T(8,128)S(1)}, u32[]{:S(2)}, u32[]{:S(2)}) %collective-permute-start.13) | collective-permute-done | bytes 655392 | tf_op jit(solution)/shard_map/ppermute | solution.py:29
  133.1 1.8 collective-permute-start.6
  134.8 0.0 collective-permute-done.12
  134.9 1.0 collective-permute-start.14
  135.9 0.0 collective-permute-done.4
  135.9 0.8 collective-permute-start.15
  136.7 0.2 fusion.93
  137.0 10.1 %collective-permute-done.3 = f32[32,1,40,128]{3,0,2,1:T(8,128)S(1)} collective-permute-done((f32[32,1,40,128]{3,0,2,1:T(8,128)S(1)}, f32[32,1,40,128]{3,0,2,1:T(8,128)S(1)}, u32[]{:S(2)}, u32[]{:S(2)}) %collective-permute-start.3) | collective-permute-done | bytes 655392 | tf_op jit(solution)/shard_map/ppermute | solution.py:29
  147.1 0.8 pad_maximum_fusion.49
  147.9 1.6 collective-permute-start.5
  149.4 0.2 collective-permute-start.7
  149.6 0.0 collective-permute-done.15
  149.6 22.2 %fusion.99 = (f32[32,10,40,128]{3,0,2,1:T(8,128)}, f32[32,10,40,128]{3,0,2,1:T(8,128)}) fusion(f32[4,8,10,40,128]{4,3,2,1,0:T(8,128)S(1)} %get-tuple-element.34, f32[32,10,40,128]{3,0,2,1:T(8,128)} %copy-done, f32[10,40,128]{2,1,0:T(8,128)S(1)} %get-tuple-element.43, f32[10,40,128]{2,1,0:T(8,128)S(1)} %get-tuple-element.42, ...), kind=kLoop, calls=%fused_computation.181 | loop fusion | flops 50790400 | bytes 29147136 | tf_op jit(solution)/shard_map/add | solution.py:66
  171.8 1.4 fusion.102
  173.2 0.1 collective-permute-start.17
  173.3 4.8 %collective-permute-start.16 = (f32[32,1,40,128]{3,0,2,1:T(8,128)S(1)}, f32[32,1,40,128]{3,0,2,1:T(8,128)S(1)}, u32[]{:S(2)}, u32[]{:S(2)}) collective-permute-start(f32[32,1,40,128]{3,0,2,1:T(8,128)S(1)} %get-tuple-element.27), channel_id=1, source_target_pairs={{4,0},{8,4},{12,8},{16,12},{20,16},{24,20},{28,24},{32,28},{36,32}... | collective-permute-start | bytes 1966088 | tf_op jit(solution)/shard_map/ppermute | solution.py:30
  178.0 0.0 collective-permute-done.5
  178.0 0.0 collective-permute-done.7
  178.0 11.9 %fusion.98 = (f32[32,10,40,128]{3,0,2,1:T(8,128)}, f32[32,10,40,128]{3,0,2,1:T(8,128)}) fusion(f32[4,8,10,40,128]{4,3,2,1,0:T(8,128)S(1)} %get-tuple-element.35, f32[32,10,40,128]{3,0,2,1:T(8,128)S(1)} %bitcast_multiply_fusion.3, f32[10,40,128]{2,1,0:T(8,128)S(1)} %get-tuple-element.43, f32[10,40,128]{2,1,0:T(8,128)S(1)} %get-tuple-element.42, ...), kind=kLoop, calls=%fused_computation.180 | loop fusion | flops 50790400 | bytes 29147136 | tf_op jit(solution)/shard_map/add | solution.py:66
  189.9 1.5 fusion.104
  191.5 0.1 collective-permute-start.9
  191.6 4.8 %collective-permute-start.8 = (f32[32,1,40,128]{3,0,2,1:T(8,128)S(1)}, f32[32,1,40,128]{3,0,2,1:T(8,128)S(1)}, u32[]{:S(2)}, u32[]{:S(2)}) collective-permute-start(f32[32,1,40,128]{3,0,2,1:T(8,128)S(1)} %get-tuple-element.31), channel_id=1, source_target_pairs={{4,0},{8,4},{12,8},{16,12},{20,16},{24,20},{28,24},{32,28},{36,32}... | collective-permute-start | bytes 1966088 | tf_op jit(solution)/shard_map/ppermute | solution.py:30
  196.3 1.0 pad_maximum_fusion.40
  197.4 1.5 collective-permute-start.18
  198.9 0.3 collective-permute-start.19
  199.2 11.0 %collective-permute-done.9 = f32[32,1,40,128]{3,0,2,1:T(8,128)S(1)} collective-permute-done((f32[32,1,40,128]{3,0,2,1:T(8,128)S(1)}, f32[32,1,40,128]{3,0,2,1:T(8,128)S(1)}, u32[]{:S(2)}, u32[]{:S(2)}) %collective-permute-start.9) | collective-permute-done | bytes 655392 | tf_op jit(solution)/shard_map/ppermute | solution.py:29
  210.3 1.9 collective-permute-start.10
  212.1 1.0 collective-permute-start.11
  213.2 13.3 %fusion.37 = f32[4,8,10,40,128]{4,1,0,3,2:T(8,128)} fusion(f32[32,10,40,128]{3,0,2,1:T(8,128)S(1)} %bitcast.35, f32[32,12,1,128]{3,0,2,1:T(8,128)S(1)} %collective-permute-done.19, f32[32,1,40,128]{3,0,2,1:T(8,128)S(1)} %collective-permute-done.16, f32[32,1,40,128]{3,0,2,1:T(8,128)S(1)} %collective-permute-done.17, ...), kind=kLoop, calls=%fused_computation.47 | loop fusion | flops 49152000 | bytes 29147136 | tf_op jit(solution)/shard_map/reshape | solution.py:89
  226.5 0.0 copy-start.4
  226.5 21.8 %fusion.17 = f32[4,8,10,40,128]{4,1,0,3,2:T(8,128)S(1)} fusion(f32[32,10,40,128]{3,0,2,1:T(8,128)} %get-tuple-element.12, f32[32,12,1,128]{3,0,2,1:T(8,128)S(1)} %collective-permute-done.11, f32[32,1,40,128]{3,0,2,1:T(8,128)S(1)} %collective-permute-done.8, f32[32,1,40,128]{3,0,2,1:T(8,128)S(1)} %collective-permute-done.9, ...), kind=kLoop, calls=%fused_computation.27 | loop fusion | flops 49152000 | bytes 29147136 | tf_op jit(solution)/shard_map/reshape | solution.py:89
  248.3 8.4 %fusion.85 = (f32[4,10,40,128]{3,2,1,0:T(8,128)}, f32[4,10,40,128]{3,2,1,0:T(8,128)}) fusion(f32[4,8,10,40,128]{4,1,0,3,2:T(8,128)S(1)} %fusion.17, f32[8,10,40,128]{3,2,1,0:T(8,128)S(1)} %copy-done.4, f32[4,8,10,40,128]{4,1,0,3,2:T(8,128)S(1)} %copy-done.2), kind=kLoop, calls=%fused_computation.133 | loop fusion | flops 6144000 | bytes 16384000 | tf_op jit(solution)/shard_map/reduce_sum | solution.py:90
  256.7 0.0 reduce-scatter.3.cloned.1.call-update
  256.7 0.0 reduce-scatter.5.cloned.1.call-start
  256.8 0.7 reduce-scatter.5.cloned.1.call-update
  257.5 27.5 %reduce-scatter.3.cloned.1.call-done = f32[1,10,40,128]{3,2,1,0:T(8,128)} async-done(((f32[4,10,40,128]{3,2,1,0:T(8,128)}), f32[1,10,40,128]{3,2,1,0:T(8,128)}) %reduce-scatter.3.cloned.1.call-update) | async-done | bytes 204816 | tf_op jit(solution)/shard_map/reduce_scatter | solution.py:91
  285.0 32.5 %reduce-scatter.5.cloned.1.call-done = f32[1,10,40,128]{3,2,1,0:T(8,128)} async-done(((f32[4,10,40,128]{3,2,1,0:T(8,128)}), f32[1,10,40,128]{3,2,1,0:T(8,128)}) %reduce-scatter.5.cloned.1.call-update) | async-done | bytes 204816 | tf_op jit(solution)/shard_map/reduce_scatter | solution.py:91
  317.5 1.8 maximum_multiply_fusion
  (43 shorter events, 0.2 us)
Async XLA Ops:
  6.5 102.7 %copy-start.3 = (f32[8,10,40,128]{3,2,1,0:T(8,128)S(1)}, f32[8,10,40,128]{3,2,1,0:T(8,128)}, u32[]{:S(2)}) copy-start(f32[8,10,40,128]{3,2,1,0:T(8,128)} %param.6) | copy-start | bytes 4915204
  6.5 11.0 %copy-start.5 = (f32[10,40,128]{2,1,0:T(8,128)S(1)}, f32[10,40,128]{2,1,0:T(8,128)}, u32[]{:S(2)}) copy-start(f32[10,40,128]{2,1,0:T(8,128)} %param.7) | copy-start | bytes 614404
  6.5 100.2 %all-reduce.7.cloned.1.call-start = ((), (), s32[]{:S(2)}) async-start(), calls=%async_computation.4 | async-start | bytes 3276800 | tf_op jit(solution)/shard_map/psum | solution.py:37
  17.5 267.5 %reduce-scatter.3.cloned.1.call-start = ((), (), s32[]{:S(2)}) async-start(), calls=%async_computation.2 | async-start | bytes 1024000 | tf_op jit(solution)/shard_map/reduce_scatter | solution.py:91
  18.2 107.8 %collective-permute-start = (f32[2,40,128]{2,1,0:T(8,128)}, f32[2,40,128]{2,1,0:T(8,128)S(1)}, u32[]{:S(2)}, u32[]{:S(2)}) collective-permute-start(f32[2,40,128]{2,1,0:T(8,128)} %get-tuple-element.44), channel_id=1, source_target_pairs={{4,0},{8,4},{12,8},{16,12},{20,16},{24,20},{28,24},{32,28},{36,32}... | collective-permute-start | bytes 122888 | tf_op jit(solution)/shard_map/ppermute | solution.py:30
  24.0 6.2 %collective-permute-start.2 = (f32[2,40,128]{2,1,0:T(8,128)S(1)}, f32[2,40,128]{2,1,0:T(8,128)S(1)}, u32[]{:S(2)}, u32[]{:S(2)}) collective-permute-start(f32[2,40,128]{2,1,0:T(8,128)S(1)} %get-tuple-element.45), channel_id=1, source_target_pairs={{0,4},{4,8},{8,12},{12,16},{16,20},{20,24},{24,28},{28,32},{32,36}... | collective-permute-start | bytes 122888 | tf_op jit(solution)/shard_map/ppermute | solution.py:29
  30.1 80.1 %copy-start.8 = (f32[14,40,128]{2,1,0:T(8,128)}, f32[14,40,128]{2,1,0:T(8,128)S(1)}, u32[]{:S(2)}) copy-start(f32[14,40,128]{2,1,0:T(8,128)S(1)} %constant_dynamic-update-slice_fusion.1) | copy-start | bytes 860164
  112.6 22.2 %copy-start = (f32[32,10,40,128]{3,0,2,1:T(8,128)}, f32[32,10,40,128]{3,0,2,1:T(8,128)S(1)}, u32[]{:S(2)}) copy-start(f32[32,10,40,128]{3,0,2,1:T(8,128)S(1)} %bitcast_multiply_fusion.1) | copy-start | bytes 19660804
  113.9 19.1 %collective-permute-start.13 = (f32[32,1,40,128]{3,0,2,1:T(8,128)}, f32[32,1,40,128]{3,0,2,1:T(8,128)S(1)}, u32[]{:S(2)}, u32[]{:S(2)}) collective-permute-start(f32[32,1,40,128]{3,0,2,1:T(8,128)} %get-tuple-element.28), channel_id=1, source_target_pairs={{0,4},{4,8},{8,12},{12,16},{16,20},{20,24},{24,28},{28,32},{32,36}... | collective-permute-start | bytes 1966088 | tf_op jit(solution)/shard_map/ppermute | solution.py:29
  115.0 19.8 %collective-permute-start.12 = (f32[32,1,40,128]{3,0,2,1:T(8,128)}, f32[32,1,40,128]{3,0,2,1:T(8,128)S(1)}, u32[]{:S(2)}, u32[]{:S(2)}) collective-permute-start(f32[32,1,40,128]{3,0,2,1:T(8,128)} %get-tuple-element.29), channel_id=1, source_target_pairs={{4,0},{8,4},{12,8},{16,12},{20,16},{24,20},{28,24},{32,28},{36,32}... | collective-permute-start | bytes 1966088 | tf_op jit(solution)/shard_map/ppermute | solution.py:30
  118.7 7.3 %copy-start.9 = (f32[14,40,128]{2,1,0:T(8,128)S(1)}, f32[14,40,128]{2,1,0:T(8,128)}, u32[]{:S(2)}) copy-start(f32[14,40,128]{2,1,0:T(8,128)} %copy-done.8) | copy-start | bytes 860164
  121.1 26.0 %collective-permute-start.3 = (f32[32,1,40,128]{3,0,2,1:T(8,128)S(1)}, f32[32,1,40,128]{3,0,2,1:T(8,128)S(1)}, u32[]{:S(2)}, u32[]{:S(2)}) collective-permute-start(f32[32,1,40,128]{3,0,2,1:T(8,128)S(1)} %get-tuple-element.32), channel_id=1, source_target_pairs={{0,4},{4,8},{8,12},{12,16},{16,20},{20,24},{24,28},{28,32},{32,36}... | collective-permute-start | bytes 1966088 | tf_op jit(solution)/shard_map/ppermute | solution.py:29
  121.2 25.9 %collective-permute-start.1 = (f32[32,1,40,128]{3,0,2,1:T(8,128)S(1)}, f32[32,1,40,128]{3,0,2,1:T(8,128)S(1)}, u32[]{:S(2)}, u32[]{:S(2)}) collective-permute-start(f32[32,1,40,128]{3,0,2,1:T(8,128)S(1)} %get-tuple-element.33), channel_id=1, source_target_pairs={{4,0},{8,4},{12,8},{16,12},{20,16},{24,20},{28,24},{32,28},{36,32}... | collective-permute-start | bytes 1966088 | tf_op jit(solution)/shard_map/ppermute | solution.py:30
  126.0 9.9 %collective-permute-start.4 = (f32[14,2,128]{2,1,0:T(2,128)S(1)}, f32[14,2,128]{2,1,0:T(2,128)S(1)}, u32[]{:S(2)}, u32[]{:S(2)}) collective-permute-start(f32[14,2,128]{2,1,0:T(2,128)S(1)} %get-tuple-element.38), channel_id=1, source_target_pairs={{1,0},{2,1},{3,2},{0,3},{5,4},{6,5},{7,6},{4,7},{9,8},{10,9},{11,1... | collective-permute-start | bytes 43016 | tf_op jit(solution)/shard_map/ppermute | solution.py:30
  133.1 3.7 %collective-permute-start.6 = (f32[14,2,128]{2,1,0:T(2,128)S(1)}, f32[14,2,128]{2,1,0:T(2,128)S(1)}, u32[]{:S(2)}, u32[]{:S(2)}) collective-permute-start(f32[14,2,128]{2,1,0:T(2,128)S(1)} %get-tuple-element.39), channel_id=1, source_target_pairs={{0,1},{1,2},{2,3},{3,0},{4,5},{5,6},{6,7},{7,4},{8,9},{9,10},{10,1... | collective-permute-start | bytes 43016 | tf_op jit(solution)/shard_map/ppermute | solution.py:29
  134.8 1.9 copy-start.6
  134.9 14.7 %collective-permute-start.14 = (f32[32,12,1,128]{3,0,2,1:T(8,128)S(1)}, f32[32,12,1,128]{3,0,2,1:T(8,128)S(1)}, u32[]{:S(2)}, u32[]{:S(2)}) collective-permute-start(f32[32,12,1,128]{3,0,2,1:T(8,128)S(1)} %get-tuple-element.20), channel_id=1, source_target_pairs={{1,0},{2,1},{3,2},{0,3},{5,4},{6,5},{7,6},{4,7},{9,8},{10,9},{11,1... | collective-permute-start | bytes 589832 | tf_op jit(solution)/shard_map/ppermute | solution.py:30
  135.9 13.7 %collective-permute-start.15 = (f32[32,12,1,128]{3,0,2,1:T(8,128)S(1)}, f32[32,12,1,128]{3,0,2,1:T(8,128)S(1)}, u32[]{:S(2)}, u32[]{:S(2)}) collective-permute-start(f32[32,12,1,128]{3,0,2,1:T(8,128)S(1)} %get-tuple-element.21), channel_id=1, source_target_pairs={{0,1},{1,2},{2,3},{3,0},{4,5},{5,6},{6,7},{7,4},{8,9},{9,10},{10,1... | collective-permute-start | bytes 589832 | tf_op jit(solution)/shard_map/ppermute | solution.py:29
  136.7 12.9 %copy-start.7 = (f32[32,1,40,128]{3,0,2,1:T(8,128)S(1)}, f32[32,1,40,128]{3,0,2,1:T(8,128)}, u32[]{:S(2)}) copy-start(f32[32,1,40,128]{3,0,2,1:T(8,128)} %copy-done.6) | copy-start | bytes 1966084
  147.9 30.2 %collective-permute-start.5 = (f32[32,12,1,128]{3,0,2,1:T(8,128)}, f32[32,12,1,128]{3,0,2,1:T(8,128)S(1)}, u32[]{:S(2)}, u32[]{:S(2)}) collective-permute-start(f32[32,12,1,128]{3,0,2,1:T(8,128)} %get-tuple-element.24), channel_id=1, source_target_pairs={{1,0},{2,1},{3,2},{0,3},{5,4},{6,5},{7,6},{4,7},{9,8},{10,9},{11,1... | collective-permute-start | bytes 589832 | tf_op jit(solution)/shard_map/ppermute | solution.py:30
  149.4 28.6 %collective-permute-start.7 = (f32[32,12,1,128]{3,0,2,1:T(8,128)}, f32[32,12,1,128]{3,0,2,1:T(8,128)S(1)}, u32[]{:S(2)}, u32[]{:S(2)}) collective-permute-start(f32[32,12,1,128]{3,0,2,1:T(8,128)} %get-tuple-element.25), channel_id=1, source_target_pairs={{0,1},{1,2},{2,3},{3,0},{4,5},{5,6},{6,7},{7,4},{8,9},{9,10},{10,1... | collective-permute-start | bytes 589832 | tf_op jit(solution)/shard_map/ppermute | solution.py:29
  173.2 23.2 %collective-permute-start.17 = (f32[32,1,40,128]{3,0,2,1:T(8,128)S(1)}, f32[32,1,40,128]{3,0,2,1:T(8,128)S(1)}, u32[]{:S(2)}, u32[]{:S(2)}) collective-permute-start(f32[32,1,40,128]{3,0,2,1:T(8,128)S(1)} %get-tuple-element.26), channel_id=1, source_target_pairs={{0,4},{4,8},{8,12},{12,16},{16,20},{20,24},{24,28},{28,32},{32,36}... | collective-permute-start | bytes 1966088 | tf_op jit(solution)/shard_map/ppermute | solution.py:29
  173.3 23.1 %collective-permute-start.16 = (f32[32,1,40,128]{3,0,2,1:T(8,128)S(1)}, f32[32,1,40,128]{3,0,2,1:T(8,128)S(1)}, u32[]{:S(2)}, u32[]{:S(2)}) collective-permute-start(f32[32,1,40,128]{3,0,2,1:T(8,128)S(1)} %get-tuple-element.27), channel_id=1, source_target_pairs={{4,0},{8,4},{12,8},{16,12},{20,16},{24,20},{28,24},{32,28},{36,32}... | collective-permute-start | bytes 1966088 | tf_op jit(solution)/shard_map/ppermute | solution.py:30
  189.9 20.3 %copy-start.1 = (f32[32,10,40,128]{3,0,2,1:T(8,128)S(1)}, f32[32,10,40,128]{3,0,2,1:T(8,128)}, u32[]{:S(2)}) copy-start(f32[32,10,40,128]{3,0,2,1:T(8,128)} %get-tuple-element.12) | copy-start | bytes 19660804
  191.5 18.8 %collective-permute-start.9 = (f32[32,1,40,128]{3,0,2,1:T(8,128)S(1)}, f32[32,1,40,128]{3,0,2,1:T(8,128)S(1)}, u32[]{:S(2)}, u32[]{:S(2)}) collective-permute-start(f32[32,1,40,128]{3,0,2,1:T(8,128)S(1)} %get-tuple-element.30), channel_id=1, source_target_pairs={{0,4},{4,8},{8,12},{12,16},{16,20},{20,24},{24,28},{28,32},{32,36}... | collective-permute-start | bytes 1966088 | tf_op jit(solution)/shard_map/ppermute | solution.py:29
  191.5 21.6 %slice-start = ((s8[6553600]{0:T(1024)(128)(4,1)}), s8[4194304]{0:T(1024)(128)(4,1)S(1)}, s32[]{:S(2)}) async-start(s8[6553600]{0:T(1024)(128)(4,1)} %bitcast.34), calls=%async_computation.5 | async-start | bytes 8388608
  191.6 18.7 %collective-permute-start.8 = (f32[32,1,40,128]{3,0,2,1:T(8,128)S(1)}, f32[32,1,40,128]{3,0,2,1:T(8,128)S(1)}, u32[]{:S(2)}, u32[]{:S(2)}) collective-permute-start(f32[32,1,40,128]{3,0,2,1:T(8,128)S(1)} %get-tuple-element.31), channel_id=1, source_target_pairs={{4,0},{8,4},{12,8},{16,12},{20,16},{24,20},{28,24},{32,28},{36,32}... | collective-permute-start | bytes 1966088 | tf_op jit(solution)/shard_map/ppermute | solution.py:30
  197.4 15.8 %collective-permute-start.18 = (f32[32,12,1,128]{3,0,2,1:T(8,128)S(1)}, f32[32,12,1,128]{3,0,2,1:T(8,128)S(1)}, u32[]{:S(2)}, u32[]{:S(2)}) collective-permute-start(f32[32,12,1,128]{3,0,2,1:T(8,128)S(1)} %get-tuple-element.18), channel_id=1, source_target_pairs={{1,0},{2,1},{3,2},{0,3},{5,4},{6,5},{7,6},{4,7},{9,8},{10,9},{11,1... | collective-permute-start | bytes 589832 | tf_op jit(solution)/shard_map/ppermute | solution.py:30
  198.9 14.3 %slice-start.1 = ((s8[6553600]{0:T(1024)(128)(4,1)}), s8[2359296]{0:T(1024)(128)(4,1)S(1)}, s32[]{:S(2)}) async-start(s8[6553600]{0:T(1024)(128)(4,1)} %bitcast.34), calls=%async_computation.6 | async-start | bytes 4718592
  198.9 14.3 %collective-permute-start.19 = (f32[32,12,1,128]{3,0,2,1:T(8,128)S(1)}, f32[32,12,1,128]{3,0,2,1:T(8,128)S(1)}, u32[]{:S(2)}, u32[]{:S(2)}) collective-permute-start(f32[32,12,1,128]{3,0,2,1:T(8,128)S(1)} %get-tuple-element.19), channel_id=1, source_target_pairs={{0,1},{1,2},{2,3},{3,0},{4,5},{5,6},{6,7},{7,4},{8,9},{9,10},{10,1... | collective-permute-start | bytes 589832 | tf_op jit(solution)/shard_map/ppermute | solution.py:29
  210.3 16.2 %collective-permute-start.10 = (f32[32,12,1,128]{3,0,2,1:T(8,128)S(1)}, f32[32,12,1,128]{3,0,2,1:T(8,128)S(1)}, u32[]{:S(2)}, u32[]{:S(2)}) collective-permute-start(f32[32,12,1,128]{3,0,2,1:T(8,128)S(1)} %get-tuple-element.22), channel_id=1, source_target_pairs={{1,0},{2,1},{3,2},{0,3},{5,4},{6,5},{7,6},{4,7},{9,8},{10,9},{11,1... | collective-permute-start | bytes 589832 | tf_op jit(solution)/shard_map/ppermute | solution.py:30
  212.1 14.3 %collective-permute-start.11 = (f32[32,12,1,128]{3,0,2,1:T(8,128)S(1)}, f32[32,12,1,128]{3,0,2,1:T(8,128)S(1)}, u32[]{:S(2)}, u32[]{:S(2)}) collective-permute-start(f32[32,12,1,128]{3,0,2,1:T(8,128)S(1)} %get-tuple-element.23), channel_id=1, source_target_pairs={{0,1},{1,2},{2,3},{3,0},{4,5},{5,6},{6,7},{7,4},{8,9},{9,10},{10,1... | collective-permute-start | bytes 589832 | tf_op jit(solution)/shard_map/ppermute | solution.py:29
  226.5 21.8 %copy-start.2 = (f32[4,8,10,40,128]{4,1,0,3,2:T(8,128)S(1)}, f32[4,8,10,40,128]{4,1,0,3,2:T(8,128)}, u32[]{:S(2)}) copy-start(f32[4,8,10,40,128]{4,1,0,3,2:T(8,128)} %fusion.37) | copy-start | bytes 19660804
  226.5 21.8 %copy-start.4 = (f32[8,10,40,128]{3,2,1,0:T(8,128)S(1)}, f32[8,10,40,128]{3,2,1,0:T(8,128)}, u32[]{:S(2)}) copy-start(f32[8,10,40,128]{3,2,1,0:T(8,128)} %param.6) | copy-start | bytes 4915204
  256.7 60.7 %reduce-scatter.5.cloned.1.call-start = ((), (), s32[]{:S(2)}) async-start(), calls=%async_computation.3 | async-start | bytes 1024000 | tf_op jit(solution)/shard_map/reduce_scatter | solution.py:91
Sparse Core Ops, SparseCore 0:
  17.6 89.0 all-reduce.6
  256.9 28.1 reduce-scatter.2
  287.8 29.6 reduce-scatter.4
where the time goes:
time: 326 us
  waiting for transfers between devices  170 us (52%)
  other arithmetic  92.8 us (28%)
  starting transfers between devices  37.3 us (11%)
  between operations  14.7 us (5%)
  local copies, waits for them, and re-layouts  11.5 us (4%)
    psum x1, waiting for transfers between devices, broadcast(): return lax.psum(block, axis)  76.6 us
    reduce_scatter x2, waiting for transfers between devices, shards(): lax.psum_scatter(partial_terms, 'orb', scatter_dimension=0, tiled=True)  60 us
    reshape x2, other arithmetic, shards(): potential.reshape((members, resident_count) + orbitals.shape[1:])  35.1 us
    add x2, other arithmetic, smooth_iterate(): iterate = iterate + search  34 us
    ppermute x10, waiting for transfers between devices, with_halo(): before = lax.ppermute(last, axis, up)  32.2 us
    ppermute x10, starting transfers between devices, with_halo(): after = lax.ppermute(initial, axis, down)  31.8 us
    reduce_sum x1, other arithmetic, shards(): partial_terms = jnp.sum(potential * orbitals[None], axis=1)  8.42 us
  transfers between devices with their start and end apart: 23, of which 7 were waited for; matrix products, arithmetic and copies ran while one was open for 19% of the time, Pallas kernels for 0%

commit v1 on v0

v1 whole, which is shorter than its diff:
```python
import math

import jax
import jax.numpy as jnp
from jax import lax
from jax.experimental import pallas as pl
from jax.experimental.pallas import tpu as pltpu
from jax.sharding import PartitionSpec as P

MESH = pl.DeviceIdType.MESH
F32 = jnp.float32

MIXING = 0.25
LOWEST = 0.5
HIGHEST = 24.0
MID = (HIGHEST + LOWEST) / 2.0
HALF = (HIGHEST - LOWEST) / 2.0
RATIO = MID / HALF
R0 = 1.0 / RATIO
R1 = 1.0 / (2.0 * RATIO - R0)
R2 = 1.0 / (2.0 * RATIO - R1)
K1, K2 = R1 * R0, R2 * R1
S1, S2 = 2.0 * R1 / HALF, 2.0 * R2 / HALF
Q = 1.0 / MID
ALPHA, BETA = K1 * Q + S1, S1 * Q
SCALE = -MIXING * 4.0 * math.pi
C0 = SCALE * (Q + ALPHA + K2 * ALPHA + S2)
C1 = -SCALE * (BETA + K2 * BETA + S2 * (Q + ALPHA))
C2 = SCALE * S2 * BETA

GROUPS = 4
RES = 8
ORBS = 32
XS = 10
SUB = 10
ROW = 14
PAIRS = 5
BASE = 18
FIRST = BASE + 2 * ROW + 2
LEAD = 32
ROWS = 240
CHUNKS = 17
LEAD_CHUNKS = 4
COUP = (CHUNKS + LEAD_CHUNKS) * 8
STARTS = (-2, 10, 18, 30)
ORDER = (0, 4, 1, 2, 3)


def kernel(
    orb, diel, owner, slots, out,
    send, rb, sib_s, sib_r, ys, yr, ds_, db, w, wd, kx, ky, kz, dd, coup, dens, flat, ob, orr,
    s_send, r_send, l_send, s_sib, r_sib, s_y, r_y, s_x, r_x, s_xs, r_xs, s_d, r_d, l_d, s_dx, r_dx, s_o, r_o, l_o,
):
    g, gx, gy = lax.axis_index("orb"), lax.axis_index("gx"), lax.axis_index("gy")
    zl, c = gy // 2, lax.rem(gy, 2)
    home = g // 2
    mine = c == home
    part = lax.rem(g, 2)
    sibling = (g, gx, 2 * zl + 1 - c)
    left, right = (g, lax.rem(gx + 15, 16), gy), (g, lax.rem(gx + 1, 16), gy)
    down, up = (g, gx, lax.rem(gy + 3, 4)), (g, gx, lax.rem(gy + 1, 4))

    def remote(src, dst, ss, rs, to):
        return pltpu.make_async_remote_copy(
            src_ref=src, dst_ref=dst, send_sem=ss, recv_sem=rs, device_id=to, device_id_type=MESH
        )

    barrier = pltpu.get_barrier_semaphore()
    for dg in range(GROUPS):
        for dc in range(2):
            if dg or dc:
                to = (lax.rem(g + dg, GROUPS), gx, 2 * zl + (c if dc == 0 else 1 - c))
                pl.semaphore_signal(barrier, inc=1, device_id=to, device_id_type=MESH)
    across = (g, gx, lax.rem(gy + 3 + 2 * c, 4))
    for to in (left, right, across):
        pl.semaphore_signal(barrier, inc=1, device_id=to, device_id_type=MESH)
    pl.semaphore_wait(barrier, 10)

    def pack_ends(f, carry):
        for x in range(XS):
            ys[0, f, 2 * x : 2 * x + 2, :] = orb[f, x, 0:2, :]
            ys[1, f, 2 * x : 2 * x + 2, :] = orb[f, x, 38:40, :]
        return carry

    lax.fori_loop(0, RES, pack_ends, 0)
    for x in range(XS):
        ys[0, RES, 2 * x : 2 * x + 2, :] = diel[x, 0:2, :]
        ys[1, RES, 2 * x : 2 * x + 2, :] = diel[x, 38:40, :]
    to_down = remote(ys.at[0], yr.at[1], s_y.at[0], r_y.at[1], down)
    to_up = remote(ys.at[1], yr.at[0], s_y.at[1], r_y.at[0], up)
    to_down.start()
    to_up.start()

    def pack(p, which):
        def body(f, carry):
            for xx in range(2):
                x = 2 * p + xx
                at = pl.multiple_of(24 * f, 8)
                for wi in which:
                    o = 12 * xx
                    if wi == 0:
                        send[p, wi, f, o : o + 2, :] = yr[0, f, 2 * x : 2 * x + 2, :]
                        send[p, wi, f, o + 2 : o + 12, :] = orb[f, x, 0:10, :]
                    elif wi == 3:
                        send[p, wi, f, o : o + 10, :] = orb[f, x, 30:40, :]
                        send[p, wi, f, o + 10 : o + 12, :] = yr[1, f, 2 * x : 2 * x + 2, :]
                    else:
                        send[p, wi, f, o : o + 12, :] = orb[f, x, STARTS[wi] : STARTS[wi] + 12, :]
            return carry

        lax.fori_loop(0, RES, body, 0)

    def share_copy(p, wi):
        to = (2 * c + wi // 2, gx, 2 * zl + wi % 2)
        here = jnp.logical_and(to[0] == g, c == wi % 2)
        away = remote(send.at[p, wi], rb.at[p + 1, g], s_send.at[p, wi], r_send.at[p, g], to)
        near = pltpu.make_async_copy(send.at[p, wi], rb.at[p + 1, g], l_send.at[p])
        return here, away, near

    def share_start(p, wi):
        here, away, near = share_copy(p, wi)
        pl.when(here)(near.start)
        pl.when(jnp.logical_not(here))(away.start)

    def share_sent(p, wi):
        here, away, near = share_copy(p, wi)
        pl.when(jnp.logical_not(here))(away.wait_send)

    def share_arrived(p, source):
        near_one = jnp.logical_and(g == source, mine)
        near = pltpu.make_async_copy(send.at[p, 0], rb.at[p + 1, source], l_send.at[p])
        away = remote(send.at[p, 0], rb.at[p + 1, source], s_send.at[p, 0], r_send.at[p, source], sibling)
        pl.when(near_one)(near.wait)
        pl.when(jnp.logical_not(near_one))(away.wait_recv)

    for p in ORDER[:2]:
        pack(p, (1, 2))
        share_start(p, 1)
        share_start(p, 2)
    to_down.wait()
    to_up.wait()
    for p in ORDER[:2]:
        pack(p, (0, 3))
        share_start(p, 0)
        share_start(p, 3)

    for ch in range(2):
        for ph in range(2):

            @pl.when(jnp.logical_and(mine, jnp.logical_and(c == ch, part == ph)))
            def _():
                for k in range(2):
                    wi = 2 * ph + k
                    for x in range(XS):
                        p, o = x // 2, ROW * (x % 2)
                        if wi == 0:
                            ds_[k, p, o : o + 2, :] = yr[0, RES, 2 * x : 2 * x + 2, :]
                            ds_[k, p, o + 2 : o + 14, :] = diel[x, 0:12, :]
                        elif wi == 3:
                            ds_[k, p, o : o + 12, :] = diel[x, 28:40, :]
                            ds_[k, p, o + 12 : o + 14, :] = yr[1, RES, 2 * x : 2 * x + 2, :]
                        else:
                            ds_[k, p, o : o + 14, :] = diel[x, 10 * wi - 2 : 10 * wi + 12, :]
                near = pltpu.make_async_copy(ds_.at[ch], db.at[pl.ds(1, PAIRS)], l_d)
                away = remote(ds_.at[1 - ch], db.at[pl.ds(1, PAIRS)], s_d, r_d, sibling)
                near.start()
                away.start()
                near.wait()
                away.wait_send()

    for p in ORDER[2:]:
        pack(p, (0, 1, 2, 3))
        for wi in range(4):
            share_start(p, wi)

    @pl.when(jnp.logical_not(mine))
    def _():
        remote(ds_.at[0], db.at[pl.ds(1, PAIRS)], s_d, r_d, sibling).wait_recv()

    d_left = remote(db.at[1], db.at[6], s_dx.at[0], r_dx.at[0], left)
    d_right = remote(db.at[5], db.at[0], s_dx.at[1], r_dx.at[1], right)
    d_left.start()
    d_right.start()
    d_left.wait()
    d_right.wait()
    wd[...] = jnp.zeros_like(wd)
    for s in range(7):
        wd[BASE + 28 * s : BASE + 28 * s + 28, :] = db[s, 0:28, :]

    lane = lax.broadcasted_iota(jnp.int32, (8, 128), 1)
    top, bottom = lane == 127, lane == 0

    def ahead(v, n=1):
        return pltpu.roll(v, 128 - n, 1)

    def at(ref, r, n=0):
        return ref[r + n : r + n + 8, :]

    for i in range(29):
        r = 8 * i
        if r + 14 + 8 > ROWS:
            break
        e, ex, ey = at(wd, r), at(wd, r, 14), at(wd, r, 1)
        kx[r : r + 8, :] = 0.5 * (e + ex)
        ky[r : r + 8, :] = 0.5 * (e + ey)
        kz[r : r + 8, :] = jnp.where(top, 0.0, 0.5 * (e + ahead(e)))

    def squared(r):
        e = at(wd, r)
        x1, x0, y1, y0 = at(kx, r), at(kx, r, -14), at(ky, r), at(ky, r, -1)
        z1 = at(kz, r)
        z0 = pltpu.roll(z1, 1, 1)
        ends = jnp.where(jnp.logical_or(top, bottom), e, 0.0)
        total = x1 + x0 + y1 + y0 + z1 + z0 + ends
        squares = x1 * x1 + x0 * x0 + y1 * y1 + y0 * y0 + z1 * z1 + z0 * z0
        return total, squares

    for i in range(2, 27):
        r = 8 * i
        total, squares = squared(r)
        dd[0, r : r + 8, :] = total
        dd[1, r : r + 8, :] = squares

    def couplings(k):
        r = FIRST + 8 * k
        d0, sq = at(dd.at[0], r), at(dd.at[1], r)
        x1, y1, z1 = at(kx, r), at(ky, r), at(kz, r)
        dx, dy = at(dd.at[0], r, 14), at(dd.at[0], r, 1)
        xx, yx, zx = at(kx, r, 14), at(ky, r, 14), at(kz, r, 14)
        xy, yy, zy = at(kx, r, 1), at(ky, r, 1), at(kz, r, 1)
        dz, xz, yz, zz = ahead(d0), ahead(x1), ahead(y1), ahead(z1)
        values = (
            C0 + C1 * d0 + C2 * (d0 * d0 + sq),
            -x1 * (C1 + C2 * (d0 + dx)),
            -y1 * (C1 + C2 * (d0 + dy)),
            -z1 * (C1 + C2 * (d0 + dz)),
            C2 * (x1 * xx),
            C2 * (y1 * yy),
            C2 * (z1 * zz),
            C2 * (x1 * yx + y1 * xy),
            C2 * (x1 * y1 + xy * yx),
            C2 * (x1 * zx + z1 * xz),
            C2 * (x1 * z1 + xz * zx),
            C2 * (y1 * zy + z1 * yz),
            C2 * (y1 * z1 + yz * zy),
        )
        for n, v in enumerate(values):
            coup[n, LEAD + 8 * k : LEAD + 8 * k + 8, :] = v

    for k in range(-LEAD_CHUNKS, CHUNKS):
        couplings(k)

    def sib_copy(p):
        return remote(sib_s.at[p], sib_r.at[p + 1], s_sib.at[p], r_sib.at[p], sibling)

    def arrive(p):
        for source in range(GROUPS):
            share_arrived(p, source)
        for ch in range(2):

            @pl.when(c == ch)
            def _():
                def body(o, carry):
                    q, f = o // RES, lax.rem(o, RES)
                    for xx in range(2):
                        a = 12 * xx + (10 if ch == 0 else 0)
                        sib_s[p, o, 2 * xx : 2 * xx + 2, :] = rb[p + 1, q, f, a : a + 2, :]
                    return carry

                lax.fori_loop(0, ORBS, body, 0)

        sib_copy(p).start()

    def edge_copies(p):
        to, slot, n = (left, 6, 0) if p == 0 else (right, 0, 1)
        return (
            remote(rb.at[p + 1], rb.at[slot], s_x.at[n], r_x.at[n], to),
            remote(sib_r.at[p + 1], sib_r.at[slot], s_xs.at[n], r_xs.at[n], to),
        )

    def unpack(slot):
        for ch in range(2):

            @pl.when(c == ch)
            def _():
                def body(o, carry):
                    q, f = o // RES, lax.rem(o, RES)
                    for xx in range(2):
                        r = BASE + 28 * slot + ROW * xx
                        m = r + (0 if ch == 0 else 2)
                        h = r + (12 if ch == 0 else 0)
                        w[o, m : m + 12, :] = rb[slot, q, f, 12 * xx : 12 * xx + 12, :]
                        w[o, h : h + 2, :] = sib_r[slot, o, 2 * xx : 2 * xx + 2, :]
                    return carry

                lax.fori_loop(0, ORBS, body, 0)

    for p in (0, 4):
        arrive(p)
        edge_copies(p)[0].start()
    for p in (0, 4):
        sib_copy(p).wait()
        edge_copies(p)[1].start()
        unpack(p + 1)
    for p in (1, 2, 3):
        arrive(p)
        sib_copy(p).wait()
        unpack(p + 1)
    for p in (0, 4):
        for e in edge_copies(p):
            e.wait()
    unpack(0)
    unpack(6)

    def density(k):
        r = FIRST + 8 * k

        def body(o, acc):
            a, b, b2 = at(w.at[o], r), at(w.at[o], r, 14), at(w.at[o], r, 28)
            y1, y2, xy = at(w.at[o], r, 1), at(w.at[o], r, 2), at(w.at[o], r, 15)
            az, az2, bz, yz = ahead(a), ahead(a, 2), ahead(b), ahead(y1)
            terms = (
                a * a, a * b, a * y1, a * az, a * b2, a * y2, a * az2,
                a * xy, b * y1, a * bz, az * b, a * yz, az * y1,
            )
            return tuple(s + t for s, t in zip(acc, terms))

        acc = lax.fori_loop(0, ORBS, body, (jnp.zeros((8, 128), F32),) * 13, unroll=4)
        for n in range(13):
            s = slice(LEAD + 8 * k, LEAD + 8 * k + 8)
            dens[n, s, :] = coup[n, s, :] * acc[n]

    def apply(k):
        r = FIRST + 8 * k
        d = LEAD + 8 * k

        def m(n, back=0):
            return dens[n, d - back : d - back + 8, :]

        def behind(v, n=1):
            return pltpu.roll(v, n, 1)

        flat_terms = (
            (0, m(0)), (14, m(1)), (-14, m(1, 14)), (1, m(2)), (-1, m(2, 1)), (28, m(4)), (-28, m(4, 28)),
            (2, m(5)), (-2, m(5, 2)), (15, m(7)), (-15, m(7, 15)), (13, m(8, 1)), (-13, m(8, 14)),
        )
        lower = ((0, m(3)), (14, m(10)), (-14, m(9, 14)), (1, m(12)), (-1, m(11, 1)))
        upper = (
            (0, behind(m(3))), (14, behind(m(9))), (-14, behind(m(10, 14))), (1, behind(m(11))), (-1, behind(m(12, 1))),
        )
        lower2, upper2 = m(6), behind(m(6), 2)

        def body(n, carry):
            window, b = n // 4, lax.rem(n, 4)
            o = owner[window] * RES + slots[window, b]
            v = {s: w[o, r + s : r + s + 8, :] for s, _ in flat_terms}

            def dot(terms):
                total = None
                for s, coefficient in terms:
                    t = coefficient * v[s]
                    total = t if total is None else total + t
                return total

            res = dot(flat_terms) + behind(dot(lower)) + ahead(dot(upper))
            res = res + behind(lower2 * v[0], 2) + ahead(upper2 * v[0], 2)
            flat[n, 8 * k : 8 * k + 8, :] = res
            return carry

        lax.fori_loop(0, 8, body, 0)

    for k in range(-LEAD_CHUNKS, CHUNKS):
        density(k)
    for k in range(CHUNKS):
        apply(k)

    def pack_out(j, carry):
        for window in range(2):
            for x in range(XS):
                o = 100 * window + 10 * x
                ob[j, o : o + 10, :] = flat[4 * window + j, ROW * x : ROW * x + 10, :]
        return carry

    lax.fori_loop(0, GROUPS, pack_out, 0)

    def out_copy(j):
        to = (j, gx, 2 * zl + home)
        here = jnp.logical_and(g == j, mine)
        slot = 2 * part + c
        away = remote(ob.at[j], orr.at[slot], s_o.at[j], r_o.at[slot], to)
        near = pltpu.make_async_copy(ob.at[j], orr.at[slot], l_o)
        return here, away, near

    for j in range(GROUPS):
        here, away, near = out_copy(j)
        pl.when(here)(near.start)
        pl.when(jnp.logical_not(here))(away.start)
    for wi in range(4):
        here = jnp.logical_and(2 * c + wi // 2 == g, c == wi % 2)
        away = remote(ob.at[0], orr.at[wi], s_o.at[0], r_o.at[wi], sibling)
        near = pltpu.make_async_copy(ob.at[0], orr.at[wi], l_o)
        pl.when(here)(near.wait)
        pl.when(jnp.logical_not(here))(away.wait_recv)
        for window in range(2):
            for x in range(XS):
                o = 100 * window + 10 * x
                out[window, 0, x, 10 * wi : 10 * wi + 10, :] = orr[wi, o : o + 10, :]

    for p in range(PAIRS):
        for wi in range(4):
            share_sent(p, wi)
    for j in range(GROUPS):
        here, away, near = out_copy(j)
        pl.when(jnp.logical_not(here))(away.wait_send)


def shards(orbitals, dielectric, owner_group, block_slots):
    dma = pltpu.SemaphoreType.DMA
    vmem = pl.BlockSpec(memory_space=pltpu.VMEM)
    smem = pl.BlockSpec(memory_space=pltpu.SMEM)

    def buf(*shape):
        return pltpu.VMEM(shape + (128,), F32)

    return pl.pallas_call(
        kernel,
        out_shape=jax.ShapeDtypeStruct((2, 1, 10, 40, 128), F32),
        in_specs=[vmem, vmem, smem, smem],
        out_specs=vmem,
        scratch_shapes=[
            buf(PAIRS, 4, RES, 24), buf(7, GROUPS, RES, 24), buf(PAIRS, ORBS, 8), buf(7, ORBS, 8),
            buf(2, RES + 1, 24), buf(2, RES + 1, 24), buf(2, PAIRS, 32), buf(7, 32),
            buf(ORBS, ROWS), buf(ROWS), buf(ROWS), buf(ROWS), buf(ROWS), buf(2, ROWS),
            buf(13, COUP), buf(13, COUP), buf(8, CHUNKS * 8), buf(GROUPS, 200), buf(4, 200),
            dma((PAIRS, 4)), dma((PAIRS, 4)), dma((PAIRS,)),
            dma((PAIRS,)), dma((PAIRS,)), dma((2,)), dma((2,)), dma((2,)), dma((2,)), dma((2,)), dma((2,)),
            dma, dma, dma, dma((2,)), dma((2,)), dma((GROUPS,)), dma((4,)), dma,
        ],
        compiler_params=pltpu.CompilerParams(collective_id=0, has_side_effects=True, vmem_limit_bytes=40 << 20),
        cost_estimate=pl.CostEstimate(flops=60_000_000, bytes_accessed=2_500_000, transcendentals=0),
    )(orbitals, dielectric, owner_group, block_slots)


def solution(mesh):
    in_specs = (P("orb", "gx", "gy", None), P("gx", "gy", None), P(), P())
    out_specs = P(None, "orb", "gx", "gy", None)
    return jax.shard_map(shards, mesh=mesh, in_specs=in_specs, out_specs=out_specs, check_vma=False)
```

time: 326 us -> 102 us (0.31)
  waiting for transfers between devices: 170 us -> 0 us
  Pallas kernels: 0 us -> 97.5 us
  other arithmetic: 92.8 us -> 0 us
  starting transfers between devices: 37.3 us -> 0 us
  between operations: 14.7 us -> 0.01 us
  local copies, waits for them, and re-layouts: 11.5 us -> 4.45 us
    pallas_call x0 -> x1, Pallas kernels: none -> 97.5 us  [shards(): pl.pallas_call(kernel, out_shape=jax.ShapeDtypeStruct((2, 1, 10, 40, 128)...]
    psum x1 -> x0, waiting for transfers between devices: 76.6 us -> none  [broadcast(): return lax.psum(block, axis)]
    reduce_scatter x2 -> x0, waiting for transfers between devices: 60 us -> none  [shards(): lax.psum_scatter(partial_terms, 'orb', scatter_dimension=0, tiled=True)]
    ppermute x20 -> x0, starting transfers between devices: 37.2 us -> none  [the longest x10 31.8 us: with_halo(): after = lax.ppermute(initial, axis, down)]
    reshape x2 -> x0, other arithmetic: 35.1 us -> none  [shards(): potential.reshape((members, resident_count) + orbitals.shape[1:])]
    add x2 -> x0, other arithmetic: 34 us -> none  [smooth_iterate(): iterate = iterate + search]
    ppermute x20 -> x0, waiting for transfers between devices: 32.2 us -> none  [the longest x10 32.2 us: with_halo(): before = lax.ppermute(last, axis, up)]
    reduce_sum x1 -> x0, other arithmetic: 8.42 us -> none  [shards(): partial_terms = jnp.sum(potential * orbitals[None], axis=1)]
  transfers between devices with their start and end apart: 23 -> 0, of which waited for: 7 -> 0; matrix products, arithmetic and copies ran while one was open for 19% -> 0% of each run, Pallas kernels for 0% -> 0%
where the time goes in v1:
time: 102 us
  Pallas kernels  97.5 us (96%)
  local copies, waits for them, and re-layouts  4.45 us (4%)
    pallas_call x1, Pallas kernels, shards(): pl.pallas_call(kernel, out_shape=jax.ShapeDtypeStruct((2, 1, 10, 40, 128)...  97.5 us
    unnamed x9, local copies, waits for them, and re-layouts  4.45 us

profile of v1, /device:TPU:1, one launch (start us, length us, event | category | flops | bytes accessed | tf_op | source)
XLA Modules:
  0.0 101.9 jit_solution(12805372345742886901)
XLA Ops:
  0.0 0.0 copy-start
  0.0 1.4 %copy-done = f32[8,10,40,128]{3,2,1,0:T(8,128)S(1)} copy-done((f32[8,10,40,128]{3,2,1,0:T(8,128)S(1)}, f32[8,10,40,128]{3,2,1,0:T(8,128)}, u32[]{:S(2)}) %copy-start) | copy-done | bytes 1638424
  1.4 0.0 copy-start.1
  1.4 0.9 copy-done.1
  2.4 0.0 copy-start.2
  2.4 0.7 copy-done.2
  3.0 0.0 copy-start.3
  3.0 0.7 copy-done.3
  3.7 97.5 %shard_map.46 = f32[2,1,10,40,128]{4,3,2,1,0:T(8,128)S(1)} custom-call(f32[8,10,40,128]{3,2,1,0:T(8,128)S(1)} %copy-done, f32[10,40,128]{2,1,0:T(8,128)S(1)} %copy-done.1, s32[2]{0:T(128)S(1)} %copy-done.3, s32[2,4]{1,0:T(2,128)S(1)} %copy-done.2), custom_call_target="tpu_custom_call" | custom-call | flops 60000000 | bytes 2500000 | tf_op jit(solution)/shard_map/pallas_call | solution.py:425
  101.2 0.8 copy.6
Async XLA Ops:
  0.0 1.4 %copy-start = (f32[8,10,40,128]{3,2,1,0:T(8,128)S(1)}, f32[8,10,40,128]{3,2,1,0:T(8,128)}, u32[]{:S(2)}) copy-start(f32[8,10,40,128]{3,2,1,0:T(8,128)} %orb.1) | copy-start | bytes 4915204
  1.4 0.9 copy-start.1
  2.4 0.7 copy-start.2
  3.0 0.7 copy-start.3

commit v2 on v1

--- a/solution.py
+++ b/solution.py
@@ -43,12 +43,13 @@
 LEAD_CHUNKS = 4
 COUP = (CHUNKS + LEAD_CHUNKS) * 8
 STARTS = (-2, 10, 18, 30)
-ORDER = (0, 4, 1, 2, 3)
+ORDER = (0, 4, 1, 3, 2)
+PIECES = ((0, 2), (8, 2), (2, 6))
 
 
 def kernel(
-    orb, diel, owner, slots, out,
-    send, rb, sib_s, sib_r, ys, yr, ds_, db, w, wd, kx, ky, kz, dd, coup, dens, flat, ob, orr,
+    orb_in, diel_in, owner_in, slots_in, out,
+    orb, diel, owner, slots, s_in, s_small, send, rb, sib_s, sib_r, ys, yr, ds_, db, w, wz, wz2, wd, kx, ky, kz, dd, coup, dens, flat, ob0, ob1, ob2, or0, or1, or2,
     s_send, r_send, l_send, s_sib, r_sib, s_y, r_y, s_x, r_x, s_xs, r_xs, s_d, r_d, l_d, s_dx, r_dx, s_o, r_o, l_o,
 ):
     g, gx, gy = lax.axis_index("orb"), lax.axis_index("gx"), lax.axis_index("gy")
@@ -65,6 +66,18 @@
             src_ref=src, dst_ref=dst, send_sem=ss, recv_sem=rs, device_id=to, device_id_type=MESH
         )
 
+    loads = [
+        pltpu.make_async_copy(orb_in.at[:, pl.ds(2 * p, 2)], orb.at[:, pl.ds(2 * p, 2)], s_in.at[p]) for p in range(PAIRS)
+    ]
+    small = [
+        pltpu.make_async_copy(a, b, s_small.at[n])
+        for n, (a, b) in enumerate(((diel_in, diel), (owner_in, owner), (slots_in, slots)))
+    ]
+    for p in ORDER:
+        loads[p].start()
+    for copy in small:
+        copy.start()
+
     barrier = pltpu.get_barrier_semaphore()
     for dg in range(GROUPS):
         for dc in range(2):
@@ -74,6 +87,8 @@
     across = (g, gx, lax.rem(gy + 3 + 2 * c, 4))
     for to in (left, right, across):
         pl.semaphore_signal(barrier, inc=1, device_id=to, device_id_type=MESH)
+    for copy in loads + small:
+        copy.wait()
     pl.semaphore_wait(barrier, 10)
 
     def pack_ends(f, carry):
@@ -293,7 +308,118 @@
                         w[o, h : h + 2, :] = sib_r[slot, o, 2 * xx : 2 * xx + 2, :]
                     return carry
 
-                lax.fori_loop(0, ORBS, body, 0)
+                lax.fori_loop(0, ORBS, body, 0, unroll=2)
+
+        def turn(o, carry):
+            for n in range(4):
+                r = BASE + 28 * slot + 8 * n
+                v = w[o, r : r + 8, :]
+                wz[o, r : r + 8, :] = ahead(v)
+                wz2[o, r : r + 8, :] = ahead(v, 2)
+            return carry
+
+        lax.fori_loop(0, ORBS, turn, 0, unroll=4)
+
+    def density(k, carry):
+        r = pl.multiple_of(FIRST - LEAD + 8 * k, 8)
+        d = pl.multiple_of(8 * k, 8)
+
+        def body(i, acc):
+            for n in range(4):
+                o = 4 * i + n
+
+                def row(ref, shift=0):
+                    return ref[o, pl.ds(r + shift, 8), :]
+
+                a, b, b2 = row(w), row(w, 14), row(w, 28)
+                y1, y2, xy = row(w, 1), row(w, 2), row(w, 15)
+                az, az2, bz, yz = row(wz), row(wz2), row(wz, 14), row(wz, 1)
+                terms = (
+                    a * a, a * b, a * y1, a * az, a * b2, a * y2, a * az2,
+                    a * xy, b * y1, a * bz, az * b, a * yz, az * y1,
+                )
+                acc = tuple(s + t for s, t in zip(acc, terms))
+            return acc
+
+        acc = lax.fori_loop(0, ORBS // 4, body, (jnp.zeros((8, 128), F32),) * 13)
+        for n in range(13):
+            dens[n, pl.ds(d, 8), :] = coup[n, pl.ds(d, 8), :] * acc[n]
+        return carry
+
+    chosen = [owner[n // 4] * RES + slots[n // 4, n % 4] for n in range(8)]
+
+    def apply(k, carry):
+        r = pl.multiple_of(FIRST + 8 * k, 8)
+        d = pl.multiple_of(LEAD + 8 * k, 8)
+
+        def m(n, back=0):
+            return dens[n, pl.ds(d - back, 8), :]
+
+        level = (
+            (0, m(0)), (14, m(1)), (-14, m(1, 14)), (1, m(2)), (-1, m(2, 1)), (28, m(4)), (-28, m(4, 28)),
+            (2, m(5)), (-2, m(5, 2)), (15, m(7)), (-15, m(7, 15)), (13, m(8, 1)), (-13, m(8, 14)),
+        )
+        z1, z2 = m(3), m(6)
+        lower = ((0, z1), (14, m(10)), (-14, m(9, 14)), (1, m(12)), (-1, m(11, 1)))
+        upper = ((0, z1), (14, m(9)), (-14, m(10, 14)), (1, m(11)), (-1, m(12, 1)))
+        for n in range(8):
+            o = chosen[n]
+            v = {s: w[o, pl.ds(r + s, 8), :] for s, _ in level}
+
+            def total(terms):
+                while len(terms) > 1:
+                    terms = [sum(terms[i + 1 : i + 2], terms[i]) for i in range(0, len(terms), 2)]
+                return terms[0]
+
+            below = total([x * v[s] for s, x in lower])
+            res = total(
+                [x * v[s] for s, x in level]
+                + [x * wz[o, pl.ds(r + s, 8), :] for s, x in upper]
+                + [z2 * wz2[o, pl.ds(r, 8), :]]
+            )
+            res = res + pltpu.roll(below, 1, 1) + pltpu.roll(z2 * v[0], 2, 1)
+            flat[n, pl.ds(pl.multiple_of(8 * k, 8), 8), :] = res
+        return carry
+
+    def out_copy(piece, j):
+        to = (j, gx, 2 * zl + home)
+        here = jnp.logical_and(g == j, mine)
+        slot = 2 * part + c
+        source, target = (ob0, ob1, ob2)[piece], (or0, or1, or2)[piece]
+        away = remote(source.at[j], target.at[slot], s_o.at[piece, j], r_o.at[piece, slot], to)
+        near = pltpu.make_async_copy(source.at[j], target.at[slot], l_o.at[piece])
+        return here, away, near
+
+    def out_start(piece):
+        first, count = PIECES[piece]
+        source = (ob0, ob1, ob2)[piece]
+
+        def pack_out(j, carry):
+            for window in range(2):
+                for n in range(count):
+                    o, x = 10 * (count * window + n), first + n
+                    source[j, o : o + 10, :] = flat[4 * window + j, ROW * x : ROW * x + 10, :]
+            return carry
+
+        lax.fori_loop(0, GROUPS, pack_out, 0)
+        for j in range(GROUPS):
+            here, away, near = out_copy(piece, j)
+            pl.when(here)(near.start)
+            pl.when(jnp.logical_not(here))(away.start)
+
+    def out_place(piece):
+        first, count = PIECES[piece]
+        source, target = (ob0, ob1, ob2)[piece], (or0, or1, or2)[piece]
+        for wi in range(4):
+            here = jnp.logical_and(2 * c + wi // 2 == g, c == wi % 2)
+            away = remote(source.at[0], target.at[wi], s_o.at[piece, 0], r_o.at[piece, wi], sibling)
+            near = pltpu.make_async_copy(source.at[0], target.at[wi], l_o.at[piece])
+            pl.when(here)(near.wait)
+            pl.when(jnp.logical_not(here))(away.wait_recv)
+            for window in range(2):
+                for n in range(count):
+                    o = 10 * (count * window + n)
+                    out[window, 0, first + n, 10 * wi : 10 * wi + 10, :] = target[wi, o : o + 10, :]
 
     for p in (0, 4):
         arrive(p)
@@ -302,122 +428,44 @@
         sib_copy(p).wait()
         edge_copies(p)[1].start()
         unpack(p + 1)
-    for p in (1, 2, 3):
-        arrive(p)
-        sib_copy(p).wait()
-        unpack(p + 1)
+    arrive(1)
+    sib_copy(1).wait()
+    unpack(2)
     for p in (0, 4):
         for e in edge_copies(p):
             e.wait()
     unpack(0)
     unpack(6)
-
-    def density(k):
-        r = FIRST + 8 * k
-
-        def body(o, acc):
-            a, b, b2 = at(w.at[o], r), at(w.at[o], r, 14), at(w.at[o], r, 28)
-            y1, y2, xy = at(w.at[o], r, 1), at(w.at[o], r, 2), at(w.at[o], r, 15)
-            az, az2, bz, yz = ahead(a), ahead(a, 2), ahead(b), ahead(y1)
-            terms = (
-                a * a, a * b, a * y1, a * az, a * b2, a * y2, a * az2,
-                a * xy, b * y1, a * bz, az * b, a * yz, az * y1,
-            )
-            return tuple(s + t for s, t in zip(acc, terms))
-
-        acc = lax.fori_loop(0, ORBS, body, (jnp.zeros((8, 128), F32),) * 13, unroll=4)
-        for n in range(13):
-            s = slice(LEAD + 8 * k, LEAD + 8 * k + 8)
-            dens[n, s, :] = coup[n, s, :] * acc[n]
-
-    def apply(k):
-        r = FIRST + 8 * k
-        d = LEAD + 8 * k
-
-        def m(n, back=0):
-            return dens[n, d - back : d - back + 8, :]
-
-        def behind(v, n=1):
-            return pltpu.roll(v, n, 1)
-
-        flat_terms = (
-            (0, m(0)), (14, m(1)), (-14, m(1, 14)), (1, m(2)), (-1, m(2, 1)), (28, m(4)), (-28, m(4, 28)),
-            (2, m(5)), (-2, m(5, 2)), (15, m(7)), (-15, m(7, 15)), (13, m(8, 1)), (-13, m(8, 14)),
-        )
-        lower = ((0, m(3)), (14, m(10)), (-14, m(9, 14)), (1, m(12)), (-1, m(11, 1)))
-        upper = (
-            (0, behind(m(3))), (14, behind(m(9))), (-14, behind(m(10, 14))), (1, behind(m(11))), (-1, behind(m(12, 1))),
-        )
-        lower2, upper2 = m(6), behind(m(6), 2)
-
-        def body(n, carry):
-            window, b = n // 4, lax.rem(n, 4)
-            o = owner[window] * RES + slots[window, b]
-            v = {s: w[o, r + s : r + s + 8, :] for s, _ in flat_terms}
-
-            def dot(terms):
-                total = None
-                for s, coefficient in terms:
-                    t = coefficient * v[s]
-                    total = t if total is None else total + t
-                return total
-
-            res = dot(flat_terms) + behind(dot(lower)) + ahead(dot(upper))
-            res = res + behind(lower2 * v[0], 2) + ahead(upper2 * v[0], 2)
-            flat[n, 8 * k : 8 * k + 8, :] = res
-            return carry
-
-        lax.fori_loop(0, 8, body, 0)
-
-    for k in range(-LEAD_CHUNKS, CHUNKS):
-        density(k)
-    for k in range(CHUNKS):
-        apply(k)
-
-    def pack_out(j, carry):
-        for window in range(2):
-            for x in range(XS):
-                o = 100 * window + 10 * x
-                ob[j, o : o + 10, :] = flat[4 * window + j, ROW * x : ROW * x + 10, :]
-        return carry
-
-    lax.fori_loop(0, GROUPS, pack_out, 0)
-
-    def out_copy(j):
-        to = (j, gx, 2 * zl + home)
-        here = jnp.logical_and(g == j, mine)
-        slot = 2 * part + c
-        away = remote(ob.at[j], orr.at[slot], s_o.at[j], r_o.at[slot], to)
-        near = pltpu.make_async_copy(ob.at[j], orr.at[slot], l_o)
-        return here, away, near
-
-    for j in range(GROUPS):
-        here, away, near = out_copy(j)
-        pl.when(here)(near.start)
-        pl.when(jnp.logical_not(here))(away.start)
-    for wi in range(4):
-        here = jnp.logical_and(2 * c + wi // 2 == g, c == wi % 2)
-        away = remote(ob.at[0], orr.at[wi], s_o.at[0], r_o.at[wi], sibling)
-        near = pltpu.make_async_copy(ob.at[0], orr.at[wi], l_o)
-        pl.when(here)(near.wait)
-        pl.when(jnp.logical_not(here))(away.wait_recv)
-        for window in range(2):
-            for x in range(XS):
-                o = 100 * window + 10 * x
-                out[window, 0, x, 10 * wi : 10 * wi + 10, :] = orr[wi, o : o + 10, :]
+    lax.fori_loop(0, 7, density, 0)
+    lax.fori_loop(0, 3, apply, 0)
+    out_start(0)
+    arrive(3)
+    sib_copy(3).wait()
+    unpack(4)
+    lax.fori_loop(14, 21, density, 0)
+    lax.fori_loop(14, 17, apply, 0)
+    out_start(1)
+    arrive(2)
+    sib_copy(2).wait()
+    unpack(3)
+    lax.fori_loop(7, 15, density, 0)
+    lax.fori_loop(3, 14, apply, 0)
+    out_start(2)
+    for piece in range(3):
+        out_place(piece)
 
     for p in range(PAIRS):
         for wi in range(4):
             share_sent(p, wi)
-    for j in range(GROUPS):
-        here, away, near = out_copy(j)
-        pl.when(jnp.logical_not(here))(away.wait_send)
+    for piece in range(3):
+        for j in range(GROUPS):
+            here, away, near = out_copy(piece, j)
+            pl.when(jnp.logical_not(here))(away.wait_send)
 
 
 def shards(orbitals, dielectric, owner_group, block_slots):
     dma = pltpu.SemaphoreType.DMA
     vmem = pl.BlockSpec(memory_space=pltpu.VMEM)
-    smem = pl.BlockSpec(memory_space=pltpu.SMEM)
 
     def buf(*shape):
         return pltpu.VMEM(shape + (128,), F32)
@@ -425,18 +473,22 @@
     return pl.pallas_call(
         kernel,
         out_shape=jax.ShapeDtypeStruct((2, 1, 10, 40, 128), F32),
-        in_specs=[vmem, vmem, smem, smem],
+        in_specs=[pl.BlockSpec(memory_space=pl.ANY)] * 4,
         out_specs=vmem,
         scratch_shapes=[
+            buf(RES, XS, 40), buf(XS, 40), pltpu.SMEM((2,), jnp.int32), pltpu.SMEM((2, 4), jnp.int32),
+            dma((PAIRS,)), dma((3,)),
             buf(PAIRS, 4, RES, 24), buf(7, GROUPS, RES, 24), buf(PAIRS, ORBS, 8), buf(7, ORBS, 8),
             buf(2, RES + 1, 24), buf(2, RES + 1, 24), buf(2, PAIRS, 32), buf(7, 32),
-            buf(ORBS, ROWS), buf(ROWS), buf(ROWS), buf(ROWS), buf(ROWS), buf(2, ROWS),
-            buf(13, COUP), buf(13, COUP), buf(8, CHUNKS * 8), buf(GROUPS, 200), buf(4, 200),
+            buf(ORBS, ROWS), buf(ORBS, ROWS), buf(ORBS, ROWS),
+            buf(ROWS), buf(ROWS), buf(ROWS), buf(ROWS), buf(2, ROWS),
+            buf(13, COUP), buf(13, COUP), buf(8, CHUNKS * 8),
+            buf(GROUPS, 40), buf(GROUPS, 40), buf(GROUPS, 120), buf(4, 40), buf(4, 40), buf(4, 120),
             dma((PAIRS, 4)), dma((PAIRS, 4)), dma((PAIRS,)),
             dma((PAIRS,)), dma((PAIRS,)), dma((2,)), dma((2,)), dma((2,)), dma((2,)), dma((2,)), dma((2,)),
-            dma, dma, dma, dma((2,)), dma((2,)), dma((GROUPS,)), dma((4,)), dma,
+            dma, dma, dma, dma((2,)), dma((2,)), dma((3, GROUPS)), dma((3, 4)), dma((3,)),
         ],
-        compiler_params=pltpu.CompilerParams(collective_id=0, has_side_effects=True, vmem_limit_bytes=40 << 20),
+        compiler_params=pltpu.CompilerParams(collective_id=0, has_side_effects=True, vmem_limit_bytes=60 << 20),
         cost_estimate=pl.CostEstimate(flops=60_000_000, bytes_accessed=2_500_000, transcendentals=0),
     )(orbitals, dielectric, owner_group, block_slots)
 

time: 102 us -> 85.5 us (0.84)
  Pallas kernels: 97.5 us -> 83.6 us
  local copies, waits for them, and re-layouts: 4.45 us -> 1.78 us
    pallas_call x1, Pallas kernels: 97.5 us -> 83.6 us  [shards(): pl.pallas_call(kernel, out_shape=jax.ShapeDtypeStruct((2, 1, 10, 40, 128)...]
    unnamed x9 -> x1, local copies, waits for them, and re-layouts: 4.45 us -> 1.78 us
where the time goes in v2:
time: 85.5 us; the launch traced here: 85.3 us
  Pallas kernels  83.6 us (98%)
  local copies, waits for them, and re-layouts  1.78 us (2%)
    pallas_call x1, Pallas kernels, shards(): pl.pallas_call(kernel, out_shape=jax.ShapeDtypeStruct((2, 1, 10, 40, 128)...  83.6 us
    unnamed x1, local copies, waits for them, and re-layouts  1.78 us

profile of v2, /device:TPU:1, one launch (start us, length us, event | category | flops | bytes accessed | tf_op | source)
XLA Modules:
  0.0 85.3 jit_solution(2174035321722506624)
XLA Ops:
  0.0 83.6 %shard_map.46 = f32[2,1,10,40,128]{4,3,2,1,0:T(8,128)} custom-call(f32[8,10,40,128]{3,2,1,0:T(8,128)} %orb_in.1, f32[10,40,128]{2,1,0:T(8,128)} %diel_in.1, s32[2]{0:T(128)} %owner_in.1, s32[2,4]{1,0:T(2,128)} %slots_in.1), custom_call_target="tpu_custom_call" | custom-call | flops 60000000 | bytes 2500000 | tf_op jit(solution)/shard_map/pallas_call | solution.py:473
  83.6 1.8 %copy.6 = f32[2,1,10,40,128]{4,3,2,1,0:T(8,128)} copy(f32[2,1,10,40,128]{4,3,2,1,0:T(8,128)} %shard_map.46) | data formatting | bytes 819200

commit v3 on v2

v3 whole, which is shorter than its diff:
```python
import math

import jax
import jax.numpy as jnp
from jax import lax
from jax.experimental import pallas as pl
from jax.experimental.pallas import tpu as pltpu
from jax.sharding import PartitionSpec as P

MESH = pl.DeviceIdType.MESH
F32 = jnp.float32

MIXING = 0.25
LOWEST = 0.5
HIGHEST = 24.0
MID = (HIGHEST + LOWEST) / 2.0
HALF = (HIGHEST - LOWEST) / 2.0
RATIO = MID / HALF
R0 = 1.0 / RATIO
R1 = 1.0 / (2.0 * RATIO - R0)
R2 = 1.0 / (2.0 * RATIO - R1)
K1, K2 = R1 * R0, R2 * R1
S1, S2 = 2.0 * R1 / HALF, 2.0 * R2 / HALF
Q = 1.0 / MID
ALPHA, BETA = K1 * Q + S1, S1 * Q
SCALE = -MIXING * 4.0 * math.pi
C0 = SCALE * (Q + ALPHA + K2 * ALPHA + S2)
C1 = -SCALE * (BETA + K2 * BETA + S2 * (Q + ALPHA))
C2 = SCALE * S2 * BETA

GROUPS = 4
RES = 8
ORBS = 32
XS = 10
SUB = 10
ROW = 14
PAIRS = 5
BASE = 18
FIRST = BASE + 2 * ROW + 2
LEAD = 32
ROWS = 240
CHUNKS = 17
LEAD_CHUNKS = 4
COUP = (CHUNKS + LEAD_CHUNKS) * 8
STARTS = (-2, 10, 18, 30)
ORDER = (0, 4, 1, 3, 2)
PIECES = (0, 8, 2, 4, 6)


def kernel(
    orb_in, diel_in, owner_in, slots_in, out,
    orb, diel, owner, slots, s_in, s_small, send, rb, sib_s, sib_r, ys, yr, ds_, db, w, wz, wz2, wd, kx, ky, kz, dd, coup, dens, flat, ob, orr,
    s_send, r_send, l_send, s_sib, r_sib, s_y, r_y, s_x, r_x, s_xs, r_xs, s_d, r_d, l_d, s_dx, r_dx, s_o, r_o, l_o,
):
    g, gx, gy = lax.axis_index("orb"), lax.axis_index("gx"), lax.axis_index("gy")
    zl, c = gy // 2, lax.rem(gy, 2)
    home = g // 2
    mine = c == home
    part = lax.rem(g, 2)
    sibling = (g, gx, 2 * zl + 1 - c)
    left, right = (g, lax.rem(gx + 15, 16), gy), (g, lax.rem(gx + 1, 16), gy)
    down, up = (g, gx, lax.rem(gy + 3, 4)), (g, gx, lax.rem(gy + 1, 4))

    def remote(src, dst, ss, rs, to):
        return pltpu.make_async_remote_copy(
            src_ref=src, dst_ref=dst, send_sem=ss, recv_sem=rs, device_id=to, device_id_type=MESH
        )

    loads = [
        pltpu.make_async_copy(orb_in.at[:, pl.ds(2 * p, 2)], orb.at[:, pl.ds(2 * p, 2)], s_in.at[p]) for p in range(PAIRS)
    ]
    small = [
        pltpu.make_async_copy(a, b, s_small.at[n])
        for n, (a, b) in enumerate(((diel_in, diel), (owner_in, owner), (slots_in, slots)))
    ]
    for p in ORDER:
        loads[p].start()
    for copy in small:
        copy.start()

    barrier = pltpu.get_barrier_semaphore()
    for dg in range(GROUPS):
        for dc in range(2):
            if dg or dc:
                to = (lax.rem(g + dg, GROUPS), gx, 2 * zl + (c if dc == 0 else 1 - c))
                pl.semaphore_signal(barrier, inc=1, device_id=to, device_id_type=MESH)
    across = (g, gx, lax.rem(gy + 3 + 2 * c, 4))
    for to in (left, right, across):
        pl.semaphore_signal(barrier, inc=1, device_id=to, device_id_type=MESH)

    def pack(p, which):
        def body(f, carry):
            for xx in range(2):
                x = 2 * p + xx
                at = pl.multiple_of(24 * f, 8)
                for wi in which:
                    o = 12 * xx
                    if wi == 0:
                        send[p, wi, f, o : o + 2, :] = yr[0, f, 2 * x : 2 * x + 2, :]
                        send[p, wi, f, o + 2 : o + 12, :] = orb[f, x, 0:10, :]
                    elif wi == 3:
                        send[p, wi, f, o : o + 10, :] = orb[f, x, 30:40, :]
                        send[p, wi, f, o + 10 : o + 12, :] = yr[1, f, 2 * x : 2 * x + 2, :]
                    else:
                        send[p, wi, f, o : o + 12, :] = orb[f, x, STARTS[wi] : STARTS[wi] + 12, :]
            return carry

        lax.fori_loop(0, RES, body, 0)

    def share_copy(p, wi):
        to = (2 * c + wi // 2, gx, 2 * zl + wi % 2)
        here = jnp.logical_and(to[0] == g, c == wi % 2)
        away = remote(send.at[p, wi], rb.at[p + 1, g], s_send.at[p, wi], r_send.at[p, g], to)
        near = pltpu.make_async_copy(send.at[p, wi], rb.at[p + 1, g], l_send.at[p])
        return here, away, near

    def share_start(p, wi):
        here, away, near = share_copy(p, wi)
        pl.when(here)(near.start)
        pl.when(jnp.logical_not(here))(away.start)

    def share_sent(p, wi):
        here, away, near = share_copy(p, wi)
        pl.when(jnp.logical_not(here))(away.wait_send)

    def share_arrived(p, source):
        near_one = jnp.logical_and(g == source, mine)
        near = pltpu.make_async_copy(send.at[p, 0], rb.at[p + 1, source], l_send.at[p])
        away = remote(send.at[p, 0], rb.at[p + 1, source], s_send.at[p, 0], r_send.at[p, source], sibling)
        pl.when(near_one)(near.wait)
        pl.when(jnp.logical_not(near_one))(away.wait_recv)

    loads[0].wait()
    pack(0, (1, 2))
    pl.semaphore_wait(barrier, 10)
    share_start(0, 1)
    share_start(0, 2)
    for copy in loads[1:] + small:
        copy.wait()

    def pack_ends(f, carry):
        for x in range(XS):
            ys[0, f, 2 * x : 2 * x + 2, :] = orb[f, x, 0:2, :]
            ys[1, f, 2 * x : 2 * x + 2, :] = orb[f, x, 38:40, :]
        return carry

    lax.fori_loop(0, RES, pack_ends, 0)
    for x in range(XS):
        ys[0, RES, 2 * x : 2 * x + 2, :] = diel[x, 0:2, :]
        ys[1, RES, 2 * x : 2 * x + 2, :] = diel[x, 38:40, :]
    to_down = remote(ys.at[0], yr.at[1], s_y.at[0], r_y.at[1], down)
    to_up = remote(ys.at[1], yr.at[0], s_y.at[1], r_y.at[0], up)
    to_down.start()
    to_up.start()

    pack(4, (1, 2))
    share_start(4, 1)
    share_start(4, 2)
    to_down.wait()
    to_up.wait()
    for ch in range(2):
        for ph in range(2):

            @pl.when(jnp.logical_and(mine, jnp.logical_and(c == ch, part == ph)))
            def _():
                for k in range(2):
                    wi = 2 * ph + k
                    for x in range(XS):
                        p, o = x // 2, ROW * (x % 2)
                        if wi == 0:
                            ds_[k, p, o : o + 2, :] = yr[0, RES, 2 * x : 2 * x + 2, :]
                            ds_[k, p, o + 2 : o + 14, :] = diel[x, 0:12, :]
                        elif wi == 3:
                            ds_[k, p, o : o + 12, :] = diel[x, 28:40, :]
                            ds_[k, p, o + 12 : o + 14, :] = yr[1, RES, 2 * x : 2 * x + 2, :]
                        else:
                            ds_[k, p, o : o + 14, :] = diel[x, 10 * wi - 2 : 10 * wi + 12, :]
                near = pltpu.make_async_copy(ds_.at[ch], db.at[pl.ds(1, PAIRS)], l_d)
                away = remote(ds_.at[1 - ch], db.at[pl.ds(1, PAIRS)], s_d, r_d, sibling)
                near.start()
                away.start()

    for p in ORDER[:2]:
        pack(p, (0, 3))
        share_start(p, 0)
        share_start(p, 3)

    for p in ORDER[2:]:
        pack(p, (0, 1, 2, 3))

    @pl.when(mine)
    def _():
        pltpu.make_async_copy(ds_.at[0], db.at[pl.ds(1, PAIRS)], l_d).wait()
        remote(ds_.at[0], db.at[pl.ds(1, PAIRS)], s_d, r_d, sibling).wait_send()

    @pl.when(jnp.logical_not(mine))
    def _():
        remote(ds_.at[0], db.at[pl.ds(1, PAIRS)], s_d, r_d, sibling).wait_recv()

    d_left = remote(db.at[1], db.at[6], s_dx.at[0], r_dx.at[0], left)
    d_right = remote(db.at[5], db.at[0], s_dx.at[1], r_dx.at[1], right)
    d_left.start()
    d_right.start()

    def sib_copy(p):
        return remote(sib_s.at[p], sib_r.at[p + 1], s_sib.at[p], r_sib.at[p], sibling)

    def arrive(p):
        for source in range(GROUPS):
            share_arrived(p, source)
        for ch in range(2):

            @pl.when(c == ch)
            def _():
                def body(o, carry):
                    q, f = o // RES, lax.rem(o, RES)
                    for xx in range(2):
                        a = 12 * xx + (10 if ch == 0 else 0)
                        sib_s[p, o, 2 * xx : 2 * xx + 2, :] = rb[p + 1, q, f, a : a + 2, :]
                    return carry

                lax.fori_loop(0, ORBS, body, 0)

        sib_copy(p).start()

    def edge_copies(p):
        to, slot, n = (left, 6, 0) if p == 0 else (right, 0, 1)
        return (
            remote(rb.at[p + 1], rb.at[slot], s_x.at[n], r_x.at[n], to),
            remote(sib_r.at[p + 1], sib_r.at[slot], s_xs.at[n], r_xs.at[n], to),
        )

    def unpack(slot):
        for ch in range(2):

            @pl.when(c == ch)
            def _():
                def body(o, carry):
                    q, f = o // RES, lax.rem(o, RES)
                    for xx in range(2):
                        r = BASE + 28 * slot + ROW * xx
                        m = r + (0 if ch == 0 else 2)
                        h = r + (12 if ch == 0 else 0)
                        w[o, m : m + 12, :] = rb[slot, q, f, 12 * xx : 12 * xx + 12, :]
                        w[o, h : h + 2, :] = sib_r[slot, o, 2 * xx : 2 * xx + 2, :]
                    return carry

                lax.fori_loop(0, ORBS, body, 0, unroll=2)

        def turn(o, carry):
            for n in range(4):
                r = BASE + 28 * slot + 8 * n
                v = w[o, r : r + 8, :]
                wz[o, r : r + 8, :] = ahead(v)
                wz2[o, r : r + 8, :] = ahead(v, 2)
            return carry

        lax.fori_loop(0, ORBS, turn, 0, unroll=4)

    def density(k, carry):
        r = pl.multiple_of(FIRST - LEAD + 8 * k, 8)
        d = pl.multiple_of(8 * k, 8)

        def body(i, acc):
            for n in range(4):
                o = 4 * i + n

                def row(ref, shift=0):
                    return ref[o, pl.ds(r + shift, 8), :]

                a, b, b2 = row(w), row(w, 14), row(w, 28)
                y1, y2, xy = row(w, 1), row(w, 2), row(w, 15)
                az, az2, bz, yz = row(wz), row(wz2), row(wz, 14), row(wz, 1)
                terms = (
                    a * a, a * b, a * y1, a * az, a * b2, a * y2, a * az2,
                    a * xy, b * y1, a * bz, az * b, a * yz, az * y1,
                )
                acc = tuple(s + t for s, t in zip(acc, terms))
            return acc

        acc = lax.fori_loop(0, ORBS // 4, body, (jnp.zeros((8, 128), F32),) * 13)
        for n in range(13):
            dens[n, pl.ds(d, 8), :] = coup[n, pl.ds(d, 8), :] * acc[n]
        return carry

    chosen = [owner[n // 4] * RES + slots[n // 4, n % 4] for n in range(8)]

    def apply(k, carry):
        r = pl.multiple_of(FIRST + 8 * k, 8)
        d = pl.multiple_of(LEAD + 8 * k, 8)

        def m(n, back=0):
            return dens[n, pl.ds(d - back, 8), :]

        level = (
            (0, m(0)), (14, m(1)), (-14, m(1, 14)), (1, m(2)), (-1, m(2, 1)), (28, m(4)), (-28, m(4, 28)),
            (2, m(5)), (-2, m(5, 2)), (15, m(7)), (-15, m(7, 15)), (13, m(8, 1)), (-13, m(8, 14)),
        )
        z1, z2 = m(3), m(6)
        lower = ((0, z1), (14, m(10)), (-14, m(9, 14)), (1, m(12)), (-1, m(11, 1)))
        upper = ((0, z1), (14, m(9)), (-14, m(10, 14)), (1, m(11)), (-1, m(12, 1)))
        for n in range(8):
            o = chosen[n]
            v = {s: w[o, pl.ds(r + s, 8), :] for s, _ in level}

            def total(terms):
                while len(terms) > 1:
                    terms = [sum(terms[i + 1 : i + 2], terms[i]) for i in range(0, len(terms), 2)]
                return terms[0]

            below = total([x * v[s] for s, x in lower])
            res = total(
                [x * v[s] for s, x in level]
                + [x * wz[o, pl.ds(r + s, 8), :] for s, x in upper]
                + [z2 * wz2[o, pl.ds(r, 8), :]]
            )
            res = res + pltpu.roll(below, 1, 1) + pltpu.roll(z2 * v[0], 2, 1)
            flat[n, pl.ds(pl.multiple_of(8 * k, 8), 8), :] = res
        return carry

    def out_copy(piece, j):
        to = (j, gx, 2 * zl + home)
        here = jnp.logical_and(g == j, mine)
        slot = 2 * part + c
        source, target = ob.at[piece], orr.at[piece]
        away = remote(source.at[j], target.at[slot], s_o.at[piece, j], r_o.at[piece, slot], to)
        near = pltpu.make_async_copy(source.at[j], target.at[slot], l_o.at[piece])
        return here, away, near

    def out_start(piece):
        first = PIECES[piece]

        def pack_out(j, carry):
            for window in range(2):
                for n in range(2):
                    o, x = 10 * (2 * window + n), first + n
                    ob[piece, j, o : o + 10, :] = flat[4 * window + j, ROW * x : ROW * x + 10, :]
            return carry

        lax.fori_loop(0, GROUPS, pack_out, 0)
        for j in range(GROUPS):
            here, away, near = out_copy(piece, j)
            pl.when(here)(near.start)
            pl.when(jnp.logical_not(here))(away.start)

    def out_place(piece):
        first = PIECES[piece]
        source, target = ob.at[piece], orr.at[piece]
        for wi in range(4):
            here = jnp.logical_and(2 * c + wi // 2 == g, c == wi % 2)
            away = remote(source.at[0], target.at[wi], s_o.at[piece, 0], r_o.at[piece, wi], sibling)
            near = pltpu.make_async_copy(source.at[0], target.at[wi], l_o.at[piece])
            pl.when(here)(near.wait)
            pl.when(jnp.logical_not(here))(away.wait_recv)
            for window in range(2):
                for n in range(2):
                    o = 10 * (2 * window + n)
                    out[window, 0, first + n, 10 * wi : 10 * wi + 10, :] = target[wi, o : o + 10, :]

    def follow(p, later):
        for wi in range(4):
            share_sent(p, wi)
        for wi in range(4):
            share_start(later, wi)

    for p, later in ((0, 1), (4, 3)):
        arrive(p)
        edge_copies(p)[0].start()
        follow(p, later)

    d_left.wait()
    d_right.wait()
    wd[...] = jnp.zeros_like(wd)
    for s in range(7):
        wd[BASE + 28 * s : BASE + 28 * s + 28, :] = db[s, 0:28, :]

    lane = lax.broadcasted_iota(jnp.int32, (8, 128), 1)
    top, bottom = lane == 127, lane == 0

    def ahead(v, n=1):
        return pltpu.roll(v, 128 - n, 1)

    def at(ref, r, n=0):
        return ref[r + n : r + n + 8, :]

    for i in range(29):
        r = 8 * i
        if r + 14 + 8 > ROWS:
            break
        e, ex, ey = at(wd, r), at(wd, r, 14), at(wd, r, 1)
        kx[r : r + 8, :] = 0.5 * (e + ex)
        ky[r : r + 8, :] = 0.5 * (e + ey)
        kz[r : r + 8, :] = jnp.where(top, 0.0, 0.5 * (e + ahead(e)))

    def squared(r):
        e = at(wd, r)
        x1, x0, y1, y0 = at(kx, r), at(kx, r, -14), at(ky, r), at(ky, r, -1)
        z1 = at(kz, r)
        z0 = pltpu.roll(z1, 1, 1)
        ends = jnp.where(jnp.logical_or(top, bottom), e, 0.0)
        total = x1 + x0 + y1 + y0 + z1 + z0 + ends
        squares = x1 * x1 + x0 * x0 + y1 * y1 + y0 * y0 + z1 * z1 + z0 * z0
        return total, squares

    for i in range(2, 27):
        r = 8 * i
        total, squares = squared(r)
        dd[0, r : r + 8, :] = total
        dd[1, r : r + 8, :] = squares

    def couplings(k):
        r = FIRST + 8 * k
        d0, sq = at(dd.at[0], r), at(dd.at[1], r)
        x1, y1, z1 = at(kx, r), at(ky, r), at(kz, r)
        dx, dy = at(dd.at[0], r, 14), at(dd.at[0], r, 1)
        xx, yx, zx = at(kx, r, 14), at(ky, r, 14), at(kz, r, 14)
        xy, yy, zy = at(kx, r, 1), at(ky, r, 1), at(kz, r, 1)
        dz, xz, yz, zz = ahead(d0), ahead(x1), ahead(y1), ahead(z1)
        values = (
            C0 + C1 * d0 + C2 * (d0 * d0 + sq),
            -x1 * (C1 + C2 * (d0 + dx)),
            -y1 * (C1 + C2 * (d0 + dy)),
            -z1 * (C1 + C2 * (d0 + dz)),
            C2 * (x1 * xx),
            C2 * (y1 * yy),
            C2 * (z1 * zz),
            C2 * (x1 * yx + y1 * xy),
            C2 * (x1 * y1 + xy * yx),
            C2 * (x1 * zx + z1 * xz),
            C2 * (x1 * z1 + xz * zx),
            C2 * (y1 * zy + z1 * yz),
            C2 * (y1 * z1 + yz * zy),
        )
        for n, v in enumerate(values):
            coup[n, LEAD + 8 * k : LEAD + 8 * k + 8, :] = v

    for k in range(-LEAD_CHUNKS, CHUNKS):
        couplings(k)

    for p in (0, 4):
        sib_copy(p).wait()
        edge_copies(p)[1].start()
        unpack(p + 1)
    arrive(1)
    follow(1, 2)
    sib_copy(1).wait()
    unpack(2)
    for p in (0, 4):
        for e in edge_copies(p):
            e.wait()
    unpack(0)
    unpack(6)
    lax.fori_loop(0, 7, density, 0)
    lax.fori_loop(0, 3, apply, 0)
    out_start(0)
    arrive(3)
    sib_copy(3).wait()
    unpack(4)
    lax.fori_loop(14, 21, density, 0)
    lax.fori_loop(14, 17, apply, 0)
    out_start(1)
    arrive(2)
    sib_copy(2).wait()
    unpack(3)
    lax.fori_loop(7, 11, density, 0)
    lax.fori_loop(3, 7, apply, 0)
    out_start(2)
    lax.fori_loop(11, 14, density, 0)
    lax.fori_loop(7, 10, apply, 0)
    out_start(3)
    lax.fori_loop(14, 15, density, 0)
    lax.fori_loop(10, 14, apply, 0)
    out_start(4)
    for piece in range(len(PIECES)):
        out_place(piece)

    for p in (3, 2):
        for wi in range(4):
            share_sent(p, wi)
    for piece in range(len(PIECES)):
        for j in range(GROUPS):
            here, away, near = out_copy(piece, j)
            pl.when(jnp.logical_not(here))(away.wait_send)


def shards(orbitals, dielectric, owner_group, block_slots):
    dma = pltpu.SemaphoreType.DMA
    vmem = pl.BlockSpec(memory_space=pltpu.VMEM)

    def buf(*shape):
        return pltpu.VMEM(shape + (128,), F32)

    return pl.pallas_call(
        kernel,
        out_shape=pltpu.VMEM((2, 1, 10, 40, 128), F32),
        in_specs=[pl.BlockSpec(memory_space=pl.ANY)] * 4,
        out_specs=vmem,
        scratch_shapes=[
            buf(RES, XS, 40), buf(XS, 40), pltpu.SMEM((2,), jnp.int32), pltpu.SMEM((2, 4), jnp.int32),
            dma((PAIRS,)), dma((3,)),
            buf(PAIRS, 4, RES, 24), buf(7, GROUPS, RES, 24), buf(PAIRS, ORBS, 8), buf(7, ORBS, 8),
            buf(2, RES + 1, 24), buf(2, RES + 1, 24), buf(2, PAIRS, 32), buf(7, 32),
            buf(ORBS, ROWS), buf(ORBS, ROWS), buf(ORBS, ROWS),
            buf(ROWS), buf(ROWS), buf(ROWS), buf(ROWS), buf(2, ROWS),
            buf(13, COUP), buf(13, COUP), buf(8, CHUNKS * 8),
            buf(5, GROUPS, 40), buf(5, 4, 40),
            dma((PAIRS, 4)), dma((PAIRS, 4)), dma((PAIRS,)),
            dma((PAIRS,)), dma((PAIRS,)), dma((2,)), dma((2,)), dma((2,)), dma((2,)), dma((2,)), dma((2,)),
            dma, dma, dma, dma((2,)), dma((2,)), dma((5, GROUPS)), dma((5, 4)), dma((5,)),
        ],
        compiler_params=pltpu.CompilerParams(collective_id=0, has_side_effects=True, vmem_limit_bytes=60 << 20),
        cost_estimate=pl.CostEstimate(flops=60_000_000, bytes_accessed=2_500_000, transcendentals=0),
    )(orbitals, dielectric, owner_group, block_slots)


def solution(mesh):
    in_specs = (P("orb", "gx", "gy", None), P("gx", "gy", None), P(), P())
    out_specs = P(None, "orb", "gx", "gy", None)
    return jax.shard_map(shards, mesh=mesh, in_specs=in_specs, out_specs=out_specs, check_vma=False)
```

time: 85.5 us -> 74.7 us (0.87)
  the two profiles are of different devices: /device:TPU:1 before, /device:TPU:36 now
where the time goes in v3:
time: 74.7 us; the launch traced here: 74.6 us
  Pallas kernels  73.9 us (99%)
  local copies, waits for them, and re-layouts  0.75 us (1%)
    pallas_call x1, Pallas kernels, shards(): pl.pallas_call(kernel, out_shape=pltpu.VMEM((2, 1, 10, 40, 128), F32), in...  73.9 us

profile of v3, /device:TPU:36, one launch (start us, length us, event | category | flops | bytes accessed | tf_op | source)
XLA Modules:
  0.0 74.6 jit_solution(18320550136822813051)
XLA Ops:
  0.0 73.9 %shard_map.46 = f32[2,1,10,40,128]{4,3,2,1,0:T(8,128)S(1)} custom-call(f32[8,10,40,128]{3,2,1,0:T(8,128)} %orb_in.1, f32[10,40,128]{2,1,0:T(8,128)} %diel_in.1, s32[2]{0:T(128)} %owner_in.1, s32[2,4]{1,0:T(2,128)} %slots_in.1), custom_call_target="tpu_custom_call" | custom-call | flops 60000000 | bytes 2500000 | tf_op jit(solution)/shard_map/pallas_call | solution.py:493
  73.9 0.8 %copy.6 = f32[2,1,10,40,128]{4,3,2,1,0:T(8,128)} copy(f32[2,1,10,40,128]{4,3,2,1,0:T(8,128)S(1)} %shard_map.46) | data formatting | bytes 819200

commit v4 on v3

--- a/solution.py
+++ b/solution.py
@@ -50,7 +50,7 @@
 def kernel(
     orb_in, diel_in, owner_in, slots_in, out,
     orb, diel, owner, slots, s_in, s_small, send, rb, sib_s, sib_r, ys, yr, ds_, db, w, wz, wz2, wd, kx, ky, kz, dd, coup, dens, flat, ob, orr,
-    s_send, r_send, l_send, s_sib, r_sib, s_y, r_y, s_x, r_x, s_xs, r_xs, s_d, r_d, l_d, s_dx, r_dx, s_o, r_o, l_o,
+    s_send, r_send, l_send, s_sib, r_sib, s_y, r_y, s_x, r_x, s_xs, r_xs, s_d, r_d, l_d, s_dx, r_dx, s_o, r_o, l_o, ready,
 ):
     g, gx, gy = lax.axis_index("orb"), lax.axis_index("gx"), lax.axis_index("gy")
     zl, c = gy // 2, lax.rem(gy, 2)
@@ -85,7 +85,7 @@
                 to = (lax.rem(g + dg, GROUPS), gx, 2 * zl + (c if dc == 0 else 1 - c))
                 pl.semaphore_signal(barrier, inc=1, device_id=to, device_id_type=MESH)
     across = (g, gx, lax.rem(gy + 3 + 2 * c, 4))
-    for to in (left, right, across):
+    for to in (left, across):
         pl.semaphore_signal(barrier, inc=1, device_id=to, device_id_type=MESH)
 
     def pack(p, which):
@@ -132,7 +132,8 @@
 
     loads[0].wait()
     pack(0, (1, 2))
-    pl.semaphore_wait(barrier, 10)
+    pl.semaphore_wait(barrier, 9)
+    pl.semaphore_signal(ready, inc=1, device_id=right, device_id_type=MESH)
     share_start(0, 1)
     share_start(0, 2)
     for copy in loads[1:] + small:
@@ -185,7 +186,10 @@
         share_start(p, 0)
         share_start(p, 3)
 
-    for p in ORDER[2:]:
+    pack(1, (0, 1, 2, 3))
+    share_start(1, 1)
+    share_start(1, 2)
+    for p in ORDER[3:]:
         pack(p, (0, 1, 2, 3))
 
     @pl.when(mine)
@@ -199,6 +203,7 @@
 
     d_left = remote(db.at[1], db.at[6], s_dx.at[0], r_dx.at[0], left)
     d_right = remote(db.at[5], db.at[0], s_dx.at[1], r_dx.at[1], right)
+    pl.semaphore_wait(ready, 1)
     d_left.start()
     d_right.start()
 
@@ -230,7 +235,11 @@
             remote(sib_r.at[p + 1], sib_r.at[slot], s_xs.at[n], r_xs.at[n], to),
         )
 
-    def unpack(slot):
+    def put(o, r, v, first, count):
+        for ref, value in ((w, v), (wz, ahead(v)), (wz2, ahead(v, 2))):
+            ref[o, r : r + count, :] = value[first : first + count]
+
+    def unpack_main(slot):
         for ch in range(2):
 
             @pl.when(c == ch)
@@ -238,24 +247,29 @@
                 def body(o, carry):
                     q, f = o // RES, lax.rem(o, RES)
                     for xx in range(2):
-                        r = BASE + 28 * slot + ROW * xx
-                        m = r + (0 if ch == 0 else 2)
-                        h = r + (12 if ch == 0 else 0)
-                        w[o, m : m + 12, :] = rb[slot, q, f, 12 * xx : 12 * xx + 12, :]
-                        w[o, h : h + 2, :] = sib_r[slot, o, 2 * xx : 2 * xx + 2, :]
+                        r = BASE + 28 * slot + ROW * xx + 2 * ch
+                        for n in (0, 4):
+                            put(o, r + n, rb[slot, q, f, 12 * xx + n : 12 * xx + n + 8, :], 0, 8)
                     return carry
 
                 lax.fori_loop(0, ORBS, body, 0, unroll=2)
 
-        def turn(o, carry):
-            for n in range(4):
-                r = BASE + 28 * slot + 8 * n
-                v = w[o, r : r + 8, :]
-                wz[o, r : r + 8, :] = ahead(v)
-                wz2[o, r : r + 8, :] = ahead(v, 2)
-            return carry
-
-        lax.fori_loop(0, ORBS, turn, 0, unroll=4)
+    def unpack_sib(slot):
+        for ch in range(2):
+
+            @pl.when(c == ch)
+            def _():
+                def body(o, carry):
+                    v = sib_r[slot, o, :, :]
+                    for xx in range(2):
+                        put(o, BASE + 28 * slot + ROW * xx + 12 * (1 - ch), v, 2 * xx, 2)
+                    return carry
+
+                lax.fori_loop(0, ORBS, body, 0, unroll=4)
+
+    def unpack(slot):
+        unpack_main(slot)
+        unpack_sib(slot)
 
     def density(k, carry):
         r = pl.multiple_of(FIRST - LEAD + 8 * k, 8)
@@ -357,16 +371,18 @@
                     o = 10 * (2 * window + n)
                     out[window, 0, first + n, 10 * wi : 10 * wi + 10, :] = target[wi, o : o + 10, :]
 
-    def follow(p, later):
-        for wi in range(4):
-            share_sent(p, wi)
-        for wi in range(4):
-            share_start(later, wi)
-
-    for p, later in ((0, 1), (4, 3)):
-        arrive(p)
-        edge_copies(p)[0].start()
-        follow(p, later)
+    arrive(0)
+    edge_copies(0)[0].start()
+    for wi in range(4):
+        share_sent(0, wi)
+    for p, wi in ((1, 0), (1, 3), (3, 1), (3, 2)):
+        share_start(p, wi)
+    arrive(4)
+    edge_copies(4)[0].start()
+    for wi in range(4):
+        share_sent(4, wi)
+    for p, wi in ((3, 0), (3, 3)):
+        share_start(p, wi)
 
     d_left.wait()
     d_right.wait()
@@ -442,9 +458,17 @@
         edge_copies(p)[1].start()
         unpack(p + 1)
     arrive(1)
-    follow(1, 2)
+    for wi in range(4):
+        share_sent(1, wi)
+    for wi in range(4):
+        share_start(2, wi)
+    unpack_main(2)
     sib_copy(1).wait()
-    unpack(2)
+    unpack_sib(2)
+    arrive(3)
+    unpack_main(4)
+    sib_copy(3).wait()
+    unpack_sib(4)
     for p in (0, 4):
         for e in edge_copies(p):
             e.wait()
@@ -452,16 +476,17 @@
     unpack(6)
     lax.fori_loop(0, 7, density, 0)
     lax.fori_loop(0, 3, apply, 0)
-    out_start(0)
-    arrive(3)
-    sib_copy(3).wait()
-    unpack(4)
     lax.fori_loop(14, 21, density, 0)
     lax.fori_loop(14, 17, apply, 0)
+    for p in (3, 2):
+        for wi in range(4):
+            share_sent(p, wi)
+    out_start(0)
     out_start(1)
     arrive(2)
+    unpack_main(3)
     sib_copy(2).wait()
-    unpack(3)
+    unpack_sib(3)
     lax.fori_loop(7, 11, density, 0)
     lax.fori_loop(3, 7, apply, 0)
     out_start(2)
@@ -474,9 +499,6 @@
     for piece in range(len(PIECES)):
         out_place(piece)
 
-    for p in (3, 2):
-        for wi in range(4):
-            share_sent(p, wi)
     for piece in range(len(PIECES)):
         for j in range(GROUPS):
             here, away, near = out_copy(piece, j)
@@ -506,7 +528,7 @@
             buf(5, GROUPS, 40), buf(5, 4, 40),
             dma((PAIRS, 4)), dma((PAIRS, 4)), dma((PAIRS,)),
             dma((PAIRS,)), dma((PAIRS,)), dma((2,)), dma((2,)), dma((2,)), dma((2,)), dma((2,)), dma((2,)),
-            dma, dma, dma, dma((2,)), dma((2,)), dma((5, GROUPS)), dma((5, 4)), dma((5,)),
+            dma, dma, dma, dma((2,)), dma((2,)), dma((5, GROUPS)), dma((5, 4)), dma((5,)), pltpu.SemaphoreType.REGULAR,
         ],
         compiler_params=pltpu.CompilerParams(collective_id=0, has_side_effects=True, vmem_limit_bytes=60 << 20),
         cost_estimate=pl.CostEstimate(flops=60_000_000, bytes_accessed=2_500_000, transcendentals=0),

time: 74.7 us -> 72 us (0.964)
  the two profiles are of different devices: /device:TPU:36 before, /device:TPU:1 now
where the time goes in v4:
time: 72 us; the launch traced here: 71.9 us
  Pallas kernels  71.1 us (99%)
  local copies, waits for them, and re-layouts  0.75 us (1%)
    pallas_call x1, Pallas kernels, shards(): pl.pallas_call(kernel, out_shape=pltpu.VMEM((2, 1, 10, 40, 128), F32), in...  71.1 us

profile of v4, /device:TPU:1, one launch (start us, length us, event | category | flops | bytes accessed | tf_op | source)
XLA Modules:
  0.0 71.9 jit_solution(14154671456569281555)
XLA Ops:
  0.0 71.1 %shard_map.46 = f32[2,1,10,40,128]{4,3,2,1,0:T(8,128)S(1)} custom-call(f32[8,10,40,128]{3,2,1,0:T(8,128)} %orb_in.1, f32[10,40,128]{2,1,0:T(8,128)} %diel_in.1, s32[2]{0:T(128)} %owner_in.1, s32[2,4]{1,0:T(2,128)} %slots_in.1), custom_call_target="tpu_custom_call" | custom-call | flops 60000000 | bytes 2500000 | tf_op jit(solution)/shard_map/pallas_call | solution.py:515
  71.1 0.8 %copy.6 = f32[2,1,10,40,128]{4,3,2,1,0:T(8,128)} copy(f32[2,1,10,40,128]{4,3,2,1,0:T(8,128)S(1)} %shard_map.46) | data formatting | bytes 819200

commit v5 on v4

--- a/solution.py
+++ b/solution.py
@@ -224,7 +224,7 @@
                         sib_s[p, o, 2 * xx : 2 * xx + 2, :] = rb[p + 1, q, f, a : a + 2, :]
                     return carry
 
-                lax.fori_loop(0, ORBS, body, 0)
+                lax.fori_loop(0, ORBS, body, 0, unroll=4)
 
         sib_copy(p).start()
 
@@ -252,7 +252,7 @@
                             put(o, r + n, rb[slot, q, f, 12 * xx + n : 12 * xx + n + 8, :], 0, 8)
                     return carry
 
-                lax.fori_loop(0, ORBS, body, 0, unroll=2)
+                lax.fori_loop(0, ORBS, body, 0, unroll=8)
 
     def unpack_sib(slot):
         for ch in range(2):
@@ -265,7 +265,7 @@
                         put(o, BASE + 28 * slot + ROW * xx + 12 * (1 - ch), v, 2 * xx, 2)
                     return carry
 
-                lax.fori_loop(0, ORBS, body, 0, unroll=4)
+                lax.fori_loop(0, ORBS, body, 0, unroll=16)
 
     def unpack(slot):
         unpack_main(slot)
@@ -375,14 +375,16 @@
     edge_copies(0)[0].start()
     for wi in range(4):
         share_sent(0, wi)
-    for p, wi in ((1, 0), (1, 3), (3, 1), (3, 2)):
-        share_start(p, wi)
+    share_start(1, 0)
+    share_start(1, 3)
     arrive(4)
     edge_copies(4)[0].start()
     for wi in range(4):
         share_sent(4, wi)
-    for p, wi in ((3, 0), (3, 3)):
-        share_start(p, wi)
+    share_start(3, 1)
+    share_start(3, 2)
+    share_start(3, 0)
+    share_start(3, 3)
 
     d_left.wait()
     d_right.wait()
@@ -460,11 +462,15 @@
     arrive(1)
     for wi in range(4):
         share_sent(1, wi)
-    for wi in range(4):
-        share_start(2, wi)
+    share_start(2, 1)
+    share_start(2, 2)
     unpack_main(2)
     sib_copy(1).wait()
     unpack_sib(2)
+    share_sent(3, 1)
+    share_sent(3, 2)
+    share_start(2, 0)
+    share_start(2, 3)
     arrive(3)
     unpack_main(4)
     sib_copy(3).wait()
@@ -478,9 +484,12 @@
     lax.fori_loop(0, 3, apply, 0)
     lax.fori_loop(14, 21, density, 0)
     lax.fori_loop(14, 17, apply, 0)
-    for p in (3, 2):
-        for wi in range(4):
-            share_sent(p, wi)
+    share_sent(3, 0)
+    share_sent(3, 3)
+    share_sent(2, 1)
+    share_sent(2, 2)
+    share_sent(2, 0)
+    share_sent(2, 3)
     out_start(0)
     out_start(1)
     arrive(2)

time: 72 us -> 70.1 us (0.974)
  Pallas kernels: 71.1 us -> 69.3 us
    pallas_call x1, Pallas kernels: 71.1 us -> 69.3 us  [shards(): pl.pallas_call(kernel, out_shape=pltpu.VMEM((2, 1, 10, 40, 128), F32), in...]
where the time goes in v5:
time: 70.1 us; the launch traced here: 70 us
  Pallas kernels  69.3 us (99%)
  local copies, waits for them, and re-layouts  0.75 us (1%)
    pallas_call x1, Pallas kernels, shards(): pl.pallas_call(kernel, out_shape=pltpu.VMEM((2, 1, 10, 40, 128), F32), in...  69.3 us

profile of v5, /device:TPU:1, one launch (start us, length us, event | category | flops | bytes accessed | tf_op | source)
XLA Modules:
  0.0 70.0 jit_solution(5244531860521639133)
XLA Ops:
  0.0 69.3 %shard_map.46 = f32[2,1,10,40,128]{4,3,2,1,0:T(8,128)S(1)} custom-call(f32[8,10,40,128]{3,2,1,0:T(8,128)} %orb_in.1, f32[10,40,128]{2,1,0:T(8,128)} %diel_in.1, s32[2]{0:T(128)} %owner_in.1, s32[2,4]{1,0:T(2,128)} %slots_in.1), custom_call_target="tpu_custom_call" | custom-call | flops 60000000 | bytes 2500000 | tf_op jit(solution)/shard_map/pallas_call | solution.py:524
  69.3 0.8 %copy.6 = f32[2,1,10,40,128]{4,3,2,1,0:T(8,128)} copy(f32[2,1,10,40,128]{4,3,2,1,0:T(8,128)S(1)} %shard_map.46) | data formatting | bytes 819200

commit v6 on v5

--- a/solution.py
+++ b/solution.py
@@ -265,7 +265,7 @@
                         put(o, BASE + 28 * slot + ROW * xx + 12 * (1 - ch), v, 2 * xx, 2)
                     return carry
 
-                lax.fori_loop(0, ORBS, body, 0, unroll=16)
+                lax.fori_loop(0, ORBS, body, 0, unroll=32)
 
     def unpack(slot):
         unpack_main(slot)

time: 70.1 us -> 70.1 us (level)
  no operation moved by 1% of the time
where the time goes in v6:
time: 70.1 us; the launch traced here: 70 us
  Pallas kernels  69.2 us (99%)
  local copies, waits for them, and re-layouts  0.75 us (1%)
    pallas_call x1, Pallas kernels, shards(): pl.pallas_call(kernel, out_shape=pltpu.VMEM((2, 1, 10, 40, 128), F32), in...  69.2 us

profile of v6, /device:TPU:1, one launch (start us, length us, event | category | flops | bytes accessed | tf_op | source)
XLA Modules:
  0.0 70.0 jit_solution(7806039553875197159)
XLA Ops:
  0.0 69.2 %shard_map.46 = f32[2,1,10,40,128]{4,3,2,1,0:T(8,128)S(1)} custom-call(f32[8,10,40,128]{3,2,1,0:T(8,128)} %orb_in.1, f32[10,40,128]{2,1,0:T(8,128)} %diel_in.1, s32[2]{0:T(128)} %owner_in.1, s32[2,4]{1,0:T(2,128)} %slots_in.1), custom_call_target="tpu_custom_call" | custom-call | flops 60000000 | bytes 2500000 | tf_op jit(solution)/shard_map/pallas_call | solution.py:524
  69.2 0.8 %copy.6 = f32[2,1,10,40,128]{4,3,2,1,0:T(8,128)} copy(f32[2,1,10,40,128]{4,3,2,1,0:T(8,128)S(1)} %shard_map.46) | data formatting | bytes 819200
